TPU v7x, 128 devices: a whole 4x4x4 slice. The times are simulated.
128 devices in a mesh: mpo: 8 (over z, core), sec: 16 (over x, y).
Axes of the slice: x: 4, y: 4, z: 4, core: 2. Of those that a mesh axis runs over, the one named last changes fastest.
Arguments:
- left_env: bfloat16 [256, 32, 384, 384], P('sec', 'mpo'), may hold values from -0.0546875 to 0.0546875
- site_tensor: bfloat16 [256, 384, 256], P('sec'), may hold values from -6 to 6
- mpo_column: bfloat16 [32, 4, 4], P('mpo'), may hold values from -3 to 3
- sector_slot: int32 [256], P('sec'), may hold values from 0 to 15, as said below
- kept: int32 [256], P('sec'), may hold values from 1 to 256
Outputs:
- expansion: bfloat16 [256, 384, 256], P('sec', 'mpo')
Inputs may be any that keep to these rules, and one draw needn't show every extreme that they name: `sector_slot`: each aligned block of 16 entries holds every slot 0 to 15 once.
All inputs are finite; a program needn't handle non-finite values.
Results may differ from a plain program's by a relative error of at most 0.0053.
Values may be sent and summed in bfloat16 or wider, within the bound.
No kernel may reach another device: no remote copies, remote signals or barrier semaphores. Data moves between devices by JAX's collectives and lax.ppermute only.
A program may use at most 128 MiB of HBM per device.

v0:
```python
import jax
import jax.numpy as jnp
from jax import lax
from jax.sharding import PartitionSpec as P

ITERS = 6


def batch_product(first, second):
    return jnp.einsum("kab,kbc->kac", first, second, precision=lax.Precision.HIGHEST)


def inverse_root(gram):
    columns = gram.shape[-1]
    frobenius = jnp.sqrt(jnp.sum(gram * gram, axis=(1, 2)))
    current = gram / frobenius[:, None, None]
    identity = jnp.broadcast_to(jnp.eye(columns, dtype=jnp.float32), gram.shape)
    partner = identity
    for repeat in range(ITERS):
        factor = 1.5 * identity - 0.5 * batch_product(partner, current)
        current = batch_product(current, factor)
        partner = batch_product(factor, partner)
    return partner / jnp.sqrt(frobenius)[:, None, None]


def shards(left_env, site_tensor, mpo_column, sector_slot, kept):
    sec_count, row_count, col_count = site_tensor.shape
    wslices, phys_dim = (mpo_column.shape[0], mpo_column.shape[1])
    right_dim = col_count // phys_dim
    shaped = site_tensor.reshape(sec_count, row_count, phys_dim, right_dim)
    mixed_site = jnp.einsum(
        "kasb,wst->kwatb", shaped, mpo_column, preferred_element_type=jnp.float32
    )
    mixed_site = mixed_site.astype(jnp.bfloat16).reshape(sec_count, wslices, row_count, col_count)
    partial_term = jnp.einsum(
        "kwab,kwbc->kac", left_env, mixed_site, preferred_element_type=jnp.float32
    )
    positions = jnp.arange(sec_count, dtype=jnp.int32)
    inverse = jnp.zeros((sec_count,), jnp.int32).at[sector_slot].set(positions)
    ordered = jnp.take(partial_term, inverse, axis=0)
    routed = lax.all_to_all(ordered, "sec", split_axis=0, concat_axis=0, tiled=True)
    owned_rows = lax.psum_scatter(routed, "mpo", scatter_dimension=1, tiled=True)
    gram_part = jnp.einsum("kac,kad->kcd", owned_rows, owned_rows, precision=lax.Precision.HIGHEST)
    gram_total = lax.psum(gram_part, "mpo")
    root_factor = inverse_root(gram_total)
    kept_mask = (jnp.arange(col_count, dtype=jnp.int32)[None, :] < kept[:, None]).astype(
        jnp.float32
    )
    result = batch_product(owned_rows, root_factor) * kept_mask[:, None, :]
    return result.astype(jnp.bfloat16)


def solution(mesh):
    return jax.shard_map(
        shards,
        mesh=mesh,
        in_specs=(
            P("sec", "mpo", None, None),
            P("sec", None, None),
            P("mpo", None, None),
            P("sec"),
            P("sec"),
        ),
        out_specs=P("sec", "mpo", None),
        check_vma=False,
    )
```

profile of v0, /device:TPU:0, one launch (start us, length us, event | category | flops | bytes accessed | tf_op | source)
XLA Modules:
  0.0 364.8 jit_solution(16589694366109846216)
XLA Ops:
  6.5 0.0 copy-start
  6.5 0.0 reduce-scatter.2.cloned.1.call-start
  6.5 0.7 compare_select_fusion.1
  7.2 0.6 scatter_custom_fusion
  7.9 3.4 copy.18
  11.3 0.0 copy-done
  11.3 7.9 %convert_bitcast_fusion = bf16[16,4,384,4,64]{2,3,4,0,1:T(4,128)(2,1)S(1)} fusion(bf16[16,384,4,64]{1,3,2,0:T(8,128)(2,1)S(1)} %bitcast.38, bf16[4,4,4]{2,1,0:T(4,128)(2,1)S(1)} %copy-done), kind=kOutput, calls=%fused_computation.2 | convolution fusion | flops 56623104 | bytes 15728768 | tf_op jit(solution)/shard_map/kasb,wst->kwatb/dot_general | solution.py:31
  19.2 7.0 %copy.21 = bf16[16,4,384,4,64]{2,4,3,1,0:T(8,128)(2,1)} copy(bf16[16,4,384,4,64]{2,3,4,0,1:T(4,128)(2,1)S(1)} %convert_bitcast_fusion) | data formatting | bytes 25165824 | tf_op jit(solution)/shard_map/convert_element_type | solution.py:34
  26.1 16.0 %convolution_bitcast_fusion = f32[16,384,256]{1,2,0:T(8,128)} fusion(bf16[16,4,384,256]{2,3,1,0:T(8,128)(2,1)} %bitcast.39, bf16[16,4,384,384]{3,2,1,0:T(8,128)(2,1)} %param.5), kind=kOutput, calls=%fused_computation.27 | convolution fusion | flops 4831838208 | bytes 37748736 | tf_op jit(solution)/shard_map/kwab,kwbc->kac/dot_general | solution.py:35
  42.2 6.4 %gather_fusion = f32[16,384,256]{1,2,0:T(8,128)} fusion(f32[16,384,256]{1,2,0:T(8,128)} %convolution_bitcast_fusion, s32[1024]{0:T(1024)S(1)} %pad_clamp_fusion), kind=kCustom, calls=%fused_computation | custom fusion | bytes 12582976 | tf_op jit(solution)/shard_map/jit(_take)/gather | solution.py:40
  48.5 3.5 broadcast_select_fusion
  52.1 80.6 %all_to_all.5 = f32[16,384,256]{1,2,0:T(8,128)} all-to-all(f32[16,384,256]{1,2,0:T(8,128)S(1)} %broadcast_select_fusion), channel_id=1, replica_groups=mesh['mpo'=8,'sec'=16] {'sec'}, dimensions={0} | all-to-all | bytes 12582912 | tf_op jit(solution)/shard_map/all_to_all | solution.py:41
  132.7 6.7 %copy.22 = f32[16,384,256]{2,0,1:T(8,128)} copy(f32[16,384,256]{1,2,0:T(8,128)} %all_to_all.5) | data formatting | bytes 12582912 | tf_op jit(solution)/shard_map/all_to_all | solution.py:41
  139.4 0.0 reduce-scatter.2.cloned.1.call-update
  139.4 0.0 copy-start.4
  139.4 0.2 all-reduce.2.cloned.1.call-start
  139.6 42.1 %reduce-scatter.2.cloned.1.call-done = f32[16,48,256]{2,0,1:T(8,128)} async-done(((f32[16,384,256]{2,0,1:T(8,128)}), f32[16,48,256]{2,0,1:T(8,128)}) %reduce-scatter.2.cloned.1.call-update) | async-done | bytes 786448 | tf_op jit(solution)/shard_map/reduce_scatter | solution.py:42
  181.8 7.6 %fusion.49 = f32[16,256,256]{2,1,0:T(8,128)} fusion(f32[16,48,256]{2,0,1:T(8,128)} %reduce-scatter.2.cloned.1.call-done), kind=kOutput, calls=%fused_computation.57 | convolution fusion | flops 603979776 | bytes 4980736 | tf_op jit(solution)/shard_map/kac,kad->kcd/dot_general | solution.py:43
  189.3 0.0 all-reduce.2.cloned.1.call-update
  189.4 0.0 copy-done.4
  189.4 0.1 fusion.54
  189.5 72.5 %all-reduce.2.cloned.1.call-done = f32[16,256,256]{2,1,0:T(8,128)} async-done(((f32[16,256,256]{2,1,0:T(8,128)}), f32[16,256,256]{2,1,0:T(8,128)}) %all-reduce.2.cloned.1.call-update) | async-done | bytes 4194320 | tf_op jit(solution)/shard_map/psum | solution.py:44
  262.0 0.0 copy-start.2
  262.0 2.8 multiply_reduce_fusion
  264.8 0.7 copy-done.2
  265.5 4.2 %fusion.30 = f32[16,256,256]{2,1,0:T(8,128)S(1)} fusion(f32[256,256]{1,0:T(8,128)S(1)} %fusion.52, f32[16,256,256]{2,1,0:T(8,128)S(1)} %copy-done.2, f32[16]{0:T(128)S(1)} %get-tuple-element.6), kind=kOutput, calls=%fused_computation.42 | convolution fusion | flops 3222274048 | bytes 8650816 | tf_op jit(solution)/shard_map/kab,kbc->kac/dot_general | solution.py:10
  269.7 4.7 %fusion.6 = f32[16,256,256]{2,1,0:T(8,128)S(1)} fusion(f32[16,256,256]{2,1,0:T(8,128)S(1)} %fusion.30, f32[256,256]{1,0:T(8,128)S(1)} %fusion.52, f32[256,256]{1,0:T(8,128)S(1)} %fusion.53), kind=kOutput, calls=%fused_computation.15 | convolution fusion | flops 3223322624 | bytes 8912896 | tf_op jit(solution)/shard_map/kab,kbc->kac/dot_general | solution.py:10
  274.4 5.2 %fusion.5 = f32[16,256,256]{2,1,0:T(8,128)S(1)} fusion(f32[16,256,256]{2,1,0:T(8,128)S(1)} %fusion.30, f32[256,256]{1,0:T(8,128)S(1)} %fusion.53, f32[16,256,256]{2,1,0:T(8,128)S(1)} %copy-done.2, f32[16]{0:T(128)S(1)} %get-tuple-element.6), kind=kOutput, calls=%fused_computation.14 | convolution fusion | flops 3224371200 | bytes 12845120 | tf_op jit(solution)/shard_map/kab,kbc->kac/dot_general | solution.py:10
  279.6 5.1 %fusion.69 = f32[16,256,256]{2,1,0:T(8,128)S(1)} fusion(f32[16,256,256]{2,1,0:T(8,128)S(1)} %fusion.6, f32[16,256,256]{2,1,0:T(8,128)S(1)} %fusion.5), kind=kOutput, calls=%fused_computation.84 | convolution fusion | flops 3221225472 | bytes 12582912 | tf_op jit(solution)/shard_map/kab,kbc->kac/dot_general | solution.py:10
  284.7 5.7 %fusion.7 = f32[16,256,256]{2,1,0:T(8,128)S(1)} fusion(f32[16,256,256]{2,1,0:T(8,128)S(1)} %fusion.5, f32[16,256,256]{2,1,0:T(8,128)S(1)} %fusion.69, f32[256,256]{1,0:T(8,128)S(1)} %fusion.53), kind=kOutput, calls=%fused_computation.16 | convolution fusion | flops 3223322624 | bytes 12845056 | tf_op jit(solution)/shard_map/kab,kbc->kac/dot_general | solution.py:10
  290.4 5.2 %fusion.8 = f32[16,256,256]{2,1,0:T(8,128)S(1)} fusion(f32[16,256,256]{2,1,0:T(8,128)S(1)} %fusion.6, f32[16,256,256]{2,1,0:T(8,128)S(1)} %fusion.69, f32[256,256]{1,0:T(8,128)S(1)} %fusion.53), kind=kOutput, calls=%fused_computation.17 | convolution fusion | flops 3223322624 | bytes 12845056 | tf_op jit(solution)/shard_map/kab,kbc->kac/dot_general | solution.py:10
  295.7 5.2 %fusion.70 = f32[16,256,256]{2,1,0:T(8,128)S(1)} fusion(f32[16,256,256]{2,1,0:T(8,128)S(1)} %fusion.8, f32[16,256,256]{2,1,0:T(8,128)S(1)} %fusion.7), kind=kOutput, calls=%fused_computation.85 | convolution fusion | flops 3221225472 | bytes 12582912 | tf_op jit(solution)/shard_map/kab,kbc->kac/dot_general | solution.py:10
  300.9 5.3 %fusion.9 = f32[16,256,256]{2,1,0:T(8,128)S(1)} fusion(f32[16,256,256]{2,1,0:T(8,128)S(1)} %fusion.7, f32[16,256,256]{2,1,0:T(8,128)S(1)} %fusion.70, f32[256,256]{1,0:T(8,128)S(1)} %fusion.53), kind=kOutput, calls=%fused_computation.18 | convolution fusion | flops 3223322624 | bytes 12845056 | tf_op jit(solution)/shard_map/kab,kbc->kac/dot_general | solution.py:10
  306.2 5.2 %fusion.10 = f32[16,256,256]{2,1,0:T(8,128)S(1)} fusion(f32[16,256,256]{2,1,0:T(8,128)S(1)} %fusion.8, f32[16,256,256]{2,1,0:T(8,128)S(1)} %fusion.70, f32[256,256]{1,0:T(8,128)S(1)} %fusion.53), kind=kOutput, calls=%fused_computation.19 | convolution fusion | flops 3223322624 | bytes 12845056 | tf_op jit(solution)/shard_map/kab,kbc->kac/dot_general | solution.py:10
  311.5 5.3 %fusion.71 = f32[16,256,256]{2,1,0:T(8,128)S(1)} fusion(f32[16,256,256]{2,1,0:T(8,128)S(1)} %fusion.10, f32[16,256,256]{2,1,0:T(8,128)S(1)} %fusion.9), kind=kOutput, calls=%fused_computation.86 | convolution fusion | flops 3221225472 | bytes 12582912 | tf_op jit(solution)/shard_map/kab,kbc->kac/dot_general | solution.py:10
  316.8 5.3 %fusion.11 = f32[16,256,256]{2,1,0:T(8,128)S(1)} fusion(f32[16,256,256]{2,1,0:T(8,128)S(1)} %fusion.9, f32[16,256,256]{2,1,0:T(8,128)S(1)} %fusion.71, f32[256,256]{1,0:T(8,128)S(1)} %fusion.53), kind=kOutput, calls=%fused_computation.20 | convolution fusion | flops 3223322624 | bytes 12845056 | tf_op jit(solution)/shard_map/kab,kbc->kac/dot_general | solution.py:10
  322.1 5.2 %fusion.12 = f32[16,256,256]{2,1,0:T(8,128)S(1)} fusion(f32[16,256,256]{2,1,0:T(8,128)S(1)} %fusion.10, f32[16,256,256]{2,1,0:T(8,128)S(1)} %fusion.71, f32[256,256]{1,0:T(8,128)S(1)} %fusion.53), kind=kOutput, calls=%fused_computation.21 | convolution fusion | flops 3223322624 | bytes 12845056 | tf_op jit(solution)/shard_map/kab,kbc->kac/dot_general | solution.py:10
  327.3 5.5 %fusion.72 = f32[16,256,256]{2,1,0:T(8,128)S(1)} fusion(f32[16,256,256]{2,1,0:T(8,128)S(1)} %fusion.12, f32[16,256,256]{2,1,0:T(8,128)S(1)} %fusion.11), kind=kOutput, calls=%fused_computation.87 | convolution fusion | flops 3221225472 | bytes 12582912 | tf_op jit(solution)/shard_map/kab,kbc->kac/dot_general | solution.py:10
  332.8 5.3 %fusion.13 = f32[16,256,256]{2,1,0:T(8,128)S(1)} fusion(f32[16,256,256]{2,1,0:T(8,128)S(1)} %fusion.11, f32[16,256,256]{2,1,0:T(8,128)S(1)} %fusion.72, f32[256,256]{1,0:T(8,128)S(1)} %fusion.53), kind=kOutput, calls=%fused_computation.22 | convolution fusion | flops 3223322624 | bytes 12845056 | tf_op jit(solution)/shard_map/kab,kbc->kac/dot_general | solution.py:10
  338.2 5.4 %fusion.14 = f32[16,256,256]{2,1,0:T(8,128)S(1)} fusion(f32[16,256,256]{2,1,0:T(8,128)S(1)} %fusion.12, f32[16,256,256]{2,1,0:T(8,128)S(1)} %fusion.72, f32[256,256]{1,0:T(8,128)S(1)} %fusion.53), kind=kOutput, calls=%fused_computation.23 | convolution fusion | flops 3223322624 | bytes 12845056 | tf_op jit(solution)/shard_map/kab,kbc->kac/dot_general | solution.py:10
  343.6 5.1 %fusion.73 = f32[16,256,256]{2,1,0:T(8,128)S(1)} fusion(f32[16,256,256]{2,1,0:T(8,128)S(1)} %fusion.14, f32[16,256,256]{2,1,0:T(8,128)S(1)} %fusion.13), kind=kOutput, calls=%fused_computation.88 | convolution fusion | flops 3221225472 | bytes 12582912 | tf_op jit(solution)/shard_map/kab,kbc->kac/dot_general | solution.py:10
  348.7 0.0 copy-start.3
  348.7 5.2 %fusion = f32[16,256,256]{2,1,0:T(8,128)S(1)} fusion(f32[16,256,256]{2,1,0:T(8,128)S(1)} %fusion.14, f32[16,256,256]{2,1,0:T(8,128)S(1)} %fusion.73, f32[256,256]{1,0:T(8,128)S(1)} %fusion.53), kind=kOutput, calls=%fused_computation.3 | convolution fusion | flops 3223322624 | bytes 12845056 | tf_op jit(solution)/shard_map/kab,kbc->kac/dot_general | solution.py:10
  353.9 0.0 copy-start.1
  353.9 0.0 copy-done.3
  353.9 3.9 %fusion.46 = bf16[16,48,256]{2,1,0:T(8,128)(2,1)} fusion(f32[16,256,256]{2,1,0:T(8,128)S(1)} %fusion, f32[16]{0:T(128)S(1)} %get-tuple-element.5, f32[16,48,256]{2,0,1:T(8,128)S(1)} %copy-done.3, f32[16,256]{1,0:T(8,128)S(1)} %fusion.54), kind=kOutput, calls=%fused_computation.56 | convolution fusion | flops 605421568 | bytes 5390400 | tf_op jit(solution)/shard_map/kab,kbc->kac/dot_general | solution.py:10
  357.8 0.0 copy-done.1
  (7 shorter events, 0.1 us)
Async XLA Ops:
  6.5 4.8 %copy-start = (bf16[4,4,4]{2,1,0:T(4,128)(2,1)S(1)}, bf16[4,4,4]{2,1,0:T(4,128)(2,1)}, u32[]{:S(2)}) copy-start(bf16[4,4,4]{2,1,0:T(4,128)(2,1)} %param.7) | copy-start | bytes 388
  6.5 175.2 %reduce-scatter.2.cloned.1.call-start = ((), (), s32[]{:S(2)}) async-start(), calls=%async_computation.2 | async-start | bytes 7077888 | tf_op jit(solution)/shard_map/reduce_scatter | solution.py:42
  139.4 50.0 %copy-start.4 = (s32[16]{0:T(128)S(1)}, s32[16]{0:T(128)}, u32[]{:S(2)}) copy-start(s32[16]{0:T(128)} %param.9) | copy-start | bytes 196
  139.4 122.6 %all-reduce.2.cloned.1.call-start = ((), (), s32[]{:S(2)}) async-start(), calls=%async_computation.3 | async-start | bytes 8388608 | tf_op jit(solution)/shard_map/psum | solution.py:44
  262.0 3.4 copy-start.2
  348.7 5.2 %copy-start.3 = (f32[16,48,256]{2,0,1:T(8,128)S(1)}, f32[16,48,256]{2,0,1:T(8,128)}, u32[]{:S(2)}) copy-start(f32[16,48,256]{2,0,1:T(8,128)} %reduce-scatter.2.cloned.1.call-done) | copy-start | bytes 2359300
  353.9 3.9 %copy-start.1 = (bf16[4,4,4]{2,1,0:T(4,128)(2,1)S(1)}, bf16[4,4,4]{2,1,0:T(4,128)(2,1)}, u32[]{:S(2)}) copy-start(bf16[4,4,4]{2,1,0:T(4,128)(2,1)} %param.7) | copy-start | bytes 388
Sparse Core Ops, SparseCore 0:
  139.5 42.2 reduce-scatter.1
  189.5 72.5 all-reduce.1
where the time goes:
time: 370 us; the launch traced here: 365 us
  matrix products  124 us (34%)
  waiting for transfers between devices  115 us (31%)
  blocking collectives  80.6 us (22%)
  local copies, waits for them, and re-layouts  24.8 us (7%)
  between operations  13.8 us (4%)
  other arithmetic  7.09 us (2%)
    dot_general x18, matrix products, batch_product(): jnp.einsum('kab,kbc->kac', first, second, precision=lax.Precision.HIGHEST)  92.2 us
    all_to_all x1, blocking collectives, shards(): lax.all_to_all(ordered, 'sec', split_axis=0, concat_axis=0, tiled=True)  80.6 us
    psum x1, waiting for transfers between devices, shards(): gram_total = lax.psum(gram_part, 'mpo')  72.5 us
    reduce_scatter x1, waiting for transfers between devices, shards(): lax.psum_scatter(routed, 'mpo', scatter_dimension=1, tiled=True)  42.1 us
    dot_general x1, matrix products, shards(): jnp.einsum('kwab,kwbc->kac', left_env, mixed_site, preferred_element_type...  16 us
    dot_general x1, matrix products, shards(): jnp.einsum('kasb,wst->kwatb', shaped, mpo_column, preferred_element_type=...  7.86 us
    dot_general x1, matrix products, shards(): jnp.einsum('kac,kad->kcd', owned_rows, owned_rows, precision=lax.Precisio...  7.57 us
  transfers between devices with their start and end apart: 2, of which 2 were waited for; matrix products, arithmetic and copies ran while one was open for 0% of the time, Pallas kernels for 0%

commit v1 on v0

v1 whole, which is shorter than its diff:
```python
import functools

import jax
import jax.numpy as jnp
from jax import lax
from jax.experimental import pallas as pl
from jax.experimental.pallas import tpu as pltpu
from jax.sharding import PartitionSpec as P

ITERS = 6
F32, BF16 = jnp.float32, jnp.bfloat16


def mixing_matrix(mpo_ref, out_ref, wslices, phys, right):
    per = 128 // right
    row = lax.broadcasted_iota(jnp.int32, (right, 128), 0)
    lane = lax.broadcasted_iota(jnp.int32, (right, 128), 1)
    for s in range(phys):
        for w in range(wslices):
            for t in range(0, phys, per):
                block = jnp.zeros((right, 128), F32)
                for p in range(per):
                    value = mpo_ref[(w * phys + s) * phys + t + p]
                    block = jnp.where(lane == row + p * right, value, block)
                column = (w * phys + t) * right
                out_ref[s * right : (s + 1) * right, column : column + 128] = block.astype(BF16)


def term_kernel(order_ref, mpo_ref, left_ref, site_ref, *rest, wslices, phys, right, adds):
    if adds:
        other_ref, out_ref, mix_ref = rest
    else:
        out_ref, mix_ref = rest
    columns = phys * right

    @pl.when(pl.program_id(0) == 0)
    def _():
        mixing_matrix(mpo_ref, mix_ref, wslices, phys, right)

    mixed = jnp.dot(site_ref[0], mix_ref[...], preferred_element_type=F32).astype(BF16)
    stacked = jnp.concatenate(
        [mixed[:, w * columns : (w + 1) * columns] for w in range(wslices)], axis=0
    )
    left = jnp.concatenate([left_ref[0, w] for w in range(wslices)], axis=1)
    term = jnp.dot(left, stacked, preferred_element_type=F32)
    if adds:
        term = term + other_ref[0].astype(F32)
    out_ref[0] = term.astype(out_ref.dtype)


def terms(order, mpo_flat, left_env, site, other, out_dtype):
    count = order.shape[0]
    _, wslices, rows, _ = left_env.shape
    columns = site.shape[2]
    phys = 4
    right = columns // phys
    in_specs = [
        pl.BlockSpec((1, wslices, rows, rows), lambda j, o, m: (o[j], 0, 0, 0)),
        pl.BlockSpec((1, rows, columns), lambda j, o, m: (o[j], 0, 0)),
    ]
    operands = [left_env, site]
    if other is not None:
        in_specs.append(pl.BlockSpec((1, rows, columns), lambda j, o, m: (j, 0, 0)))
        operands.append(other)
    flops = 2 * count * rows * columns * wslices * (rows + columns)
    moved = count * (wslices * rows * rows * 2 + rows * columns * 6)
    return pl.pallas_call(
        functools.partial(
            term_kernel, wslices=wslices, phys=phys, right=right, adds=other is not None
        ),
        out_shape=jax.ShapeDtypeStruct((count, rows, columns), out_dtype),
        grid_spec=pltpu.PrefetchScalarGridSpec(
            num_scalar_prefetch=2,
            grid=(count,),
            in_specs=in_specs,
            out_specs=pl.BlockSpec((1, rows, columns), lambda j, o, m: (j, 0, 0)),
            scratch_shapes=[pltpu.VMEM((columns, wslices * columns), BF16)],
        ),
        compiler_params=pltpu.CompilerParams(vmem_limit_bytes=24 * 2**20),
        cost_estimate=pl.CostEstimate(flops=flops, bytes_accessed=moved, transcendentals=0),
    )(order, mpo_flat, *operands)


def split(a):
    high = a.astype(BF16)
    return high, (a - high.astype(F32)).astype(BF16)


def product(a, b):
    return jnp.dot(
        jnp.concatenate([a[0], a[0], a[1]], axis=1),
        jnp.concatenate([b[0], b[1], b[0]], axis=0),
        preferred_element_type=F32,
    )


def root_kernel(own_ref, far_ref, up_ref, down_ref, out_ref):
    count, rows, columns = own_ref.shape
    parts, _, part_rows, _ = out_ref.shape
    eye = lax.broadcasted_iota(jnp.int32, (columns, columns), 0) == lax.broadcasted_iota(
        jnp.int32, (columns, columns), 1
    )
    identity = eye.astype(F32)
    sectors = range(count)
    term, current, scale = [], [], []
    for b in sectors:
        total = (
            own_ref[b]
            + far_ref[b].astype(F32)
            + up_ref[b].astype(F32)
            + down_ref[b].astype(F32)
        )
        high, low = split(total)
        gram = lax.dot_general(
            jnp.concatenate([high, high, low], axis=0),
            jnp.concatenate([high, low, high], axis=0),
            (((0,), (0,)), ((), ())),
            preferred_element_type=F32,
        )
        norm = jnp.sqrt(jnp.sum(gram * gram, keepdims=True))
        term.append((high, low))
        current.append(gram / norm)
        scale.append(1.0 / jnp.sqrt(norm))
    partner = [None] * count
    for repeat in range(ITERS):
        halves = [split(current[b]) for b in sectors]
        if repeat == 0:
            factor = [1.5 * identity - 0.5 * current[b] for b in sectors]
        else:
            others = [split(partner[b]) for b in sectors]
            factor = [1.5 * identity - 0.5 * product(others[b], halves[b]) for b in sectors]
        pairs = [split(factor[b]) for b in sectors]
        if repeat < ITERS - 1:
            current = [product(halves[b], pairs[b]) for b in sectors]
        if repeat == 0:
            partner = factor
        else:
            partner = [product(pairs[b], others[b]) for b in sectors]
    for b in sectors:
        result = (product(term[b], split(partner[b] * scale[b]))).astype(BF16)
        for m in range(parts):
            out_ref[m, b] = result[m * part_rows : (m + 1) * part_rows]


def expansions(own, far, up, down, parts):
    count, rows, columns = own.shape
    flops = 2 * 3 * count * columns * columns * (15 * columns + 2 * rows)
    return pl.pallas_call(
        root_kernel,
        out_shape=jax.ShapeDtypeStruct((parts, count, rows // parts, columns), BF16),
        in_specs=[pl.BlockSpec(memory_space=pltpu.VMEM)] * 4,
        out_specs=pl.BlockSpec(memory_space=pltpu.VMEM),
        compiler_params=pltpu.CompilerParams(vmem_limit_bytes=40 * 2**20),
        cost_estimate=pl.CostEstimate(
            flops=flops, bytes_accessed=count * rows * columns * 12, transcendentals=0
        ),
    )(own, far, up, down)


def shards(left_env, site_tensor, mpo_column, sector_slot, kept):
    columns = site_tensor.shape[2]
    members = lax.axis_size("mpo")
    chips = members // 2
    me = lax.axis_index("mpo")
    chip, core = me // 2, me % 2

    positions = jnp.arange(sector_slot.shape[0], dtype=jnp.int32)

    def order_of(targets):
        slots = jnp.stack([2 * (2 * (c % chips) + q) + b for c, q in targets for b in range(2)])
        match = sector_slot[None, :] == slots[:, None]
        return jnp.sum(jnp.where(match, positions[None, :], 0), axis=1, dtype=jnp.int32)

    mpo_flat = mpo_column.astype(F32).reshape(-1)
    other = 1 - core
    order = order_of(
        [
            (chip + 2, other),
            (chip + 1, other),
            (chip + 3, other),
            (chip + 2, core),
            (chip + 1, core),
            (chip + 3, core),
            (chip, other),
            (chip, core),
        ]
    )
    swap = [(2 * c + q, 2 * c + 1 - q) for c in range(chips) for q in range(2)]

    def shift(step):
        return [
            (2 * c + q, 2 * ((c + step) % chips) + q) for c in range(chips) for q in range(2)
        ]

    def run(first, count, recv, dtype):
        return terms(order[first : first + count], mpo_flat, left_env, site_tensor, recv, dtype)

    far_other = lax.ppermute(run(0, 2, None, BF16), "mpo", swap)
    near_other = lax.ppermute(run(2, 4, None, BF16), "mpo", swap)
    far = lax.ppermute(run(6, 2, far_other, BF16), "mpo", shift(2))
    near = run(8, 4, near_other, BF16)
    up = lax.ppermute(near[:2], "mpo", shift(1))
    down = lax.ppermute(near[2:], "mpo", shift(3))
    own_other = lax.ppermute(run(12, 2, None, BF16), "mpo", swap)
    own = run(14, 2, own_other, F32)
    result = expansions(own, far, up, down, members)
    rows = lax.all_to_all(result, "mpo", split_axis=0, concat_axis=0, tiled=True)
    rows = rows.reshape(-1, rows.shape[2], columns)
    routed = lax.all_to_all(rows, "sec", split_axis=0, concat_axis=0, tiled=True)
    keep = jnp.arange(columns, dtype=jnp.int32)[None, None, :] < kept[:, None, None]
    return jnp.where(keep, routed, jnp.zeros((), BF16))


def solution(mesh):
    return jax.shard_map(
        shards,
        mesh=mesh,
        in_specs=(
            P("sec", "mpo", None, None),
            P("sec", None, None),
            P("mpo", None, None),
            P("sec"),
            P("sec"),
        ),
        out_specs=P("sec", "mpo", None),
        check_vma=False,
    )
```

time: 370 us -> 86.7 us (0.23); the launches traced: 365 us -> 86.3 us
  matrix products: 124 us -> 0 us
  waiting for transfers between devices: 115 us -> 16.4 us
  blocking collectives: 80.6 us -> 12.8 us
  Pallas kernels: 0 us -> 29.3 us
  starting transfers between devices: 0.22 us -> 14.8 us
  local copies, waits for them, and re-layouts: 24.8 us -> 11.1 us
  between operations: 13.8 us -> 0.17 us
  other arithmetic: 7.09 us -> 1.7 us
    dot_general x21 -> x0, matrix products: 124 us -> none  [the longest x18 92.2 us: batch_product(): jnp.einsum('kab,kbc->kac', first, second, precision=lax.Precision.HIGHEST)]
    psum x1 -> x0, waiting for transfers between devices: 72.5 us -> none  [shards(): gram_total = lax.psum(gram_part, 'mpo')]
    all_to_all x1, blocking collectives: 80.6 us -> 12.8 us  [shards(): lax.all_to_all(result, 'mpo', split_axis=0, concat_axis=0, tiled=True)]
    reduce_scatter x1 -> x0, waiting for transfers between devices: 42.1 us -> none  [shards(): lax.psum_scatter(routed, 'mpo', scatter_dimension=1, tiled=True)]
    pallas_call x0 -> x7, Pallas kernels: none -> 29.3 us  [the longest x6 23.6 us: terms(): pl.pallas_call(functools.partial(term_kernel, wslices=wslices, phys=phys,...]
    all_to_all x0 -> x1, waiting for transfers between devices: none -> 9.54 us  [shards(): lax.all_to_all(rows, 'sec', split_axis=0, concat_axis=0, tiled=True)]
    ppermute x0 -> x6, starting transfers between devices: none -> 7.79 us  [the longest x1 3.96 us: shards(): far = lax.ppermute(run(6, 2, far_other, BF16), 'mpo', shift(2))]
    all_to_all x0 -> x1, starting transfers between devices: none -> 7.04 us  [shards(): lax.all_to_all(rows, 'sec', split_axis=0, concat_axis=0, tiled=True)]
  transfers between devices with their start and end apart: 2 -> 7, of which waited for: 2 -> 3; matrix products, arithmetic and copies ran while one was open for 0% -> 0% of each run, Pallas kernels for 0% -> 21%
where the time goes in v1:
time: 86.7 us; the launch traced here: 86.3 us
  Pallas kernels  29.3 us (34%)
  waiting for transfers between devices  16.4 us (19%)
  starting transfers between devices  14.8 us (17%)
  blocking collectives  12.8 us (15%)
  local copies, waits for them, and re-layouts  11.1 us (13%)
  other arithmetic  1.7 us (2%)
    pallas_call x6, Pallas kernels, terms(): pl.pallas_call(functools.partial(term_kernel, wslices=wslices, phys=phys,...  23.6 us
    all_to_all x1, blocking collectives, shards(): lax.all_to_all(result, 'mpo', split_axis=0, concat_axis=0, tiled=True)  12.8 us
    unnamed x30, local copies, waits for them, and re-layouts  10 us
    all_to_all x1, waiting for transfers between devices, shards(): lax.all_to_all(rows, 'sec', split_axis=0, concat_axis=0, tiled=True)  9.54 us
    all_to_all x1, starting transfers between devices, shards(): lax.all_to_all(rows, 'sec', split_axis=0, concat_axis=0, tiled=True)  7.04 us
    ppermute x1, waiting for transfers between devices, shards(): up = lax.ppermute(near[:2], 'mpo', shift(1))  6.12 us
    pallas_call x1, Pallas kernels, expansions(): pl.pallas_call(root_kernel, out_shape=jax.ShapeDtypeStruct((parts, count,...  5.66 us
    ppermute x1, starting transfers between devices, shards(): far = lax.ppermute(run(6, 2, far_other, BF16), 'mpo', shift(2))  3.96 us
  transfers between devices with their start and end apart: 7, of which 3 were waited for; matrix products, arithmetic and copies ran while one was open for 0% of the time, Pallas kernels for 21%

profile of v1, /device:TPU:0, one launch (start us, length us, event | category | flops | bytes accessed | tf_op | source)
XLA Modules:
  0.0 86.3 jit_solution(2314979926451325760)
XLA Ops:
  0.0 0.1 stack.67
  0.1 0.8 select_reduce_fusion
  0.9 0.1 fusion.1
  1.0 0.8 reshape.35.mpo_ref
  1.8 0.0 copy-start
  1.8 6.4 %copy-done = bf16[16,4,384,384]{3,2,1,0:T(8,128)(2,1)S(1)} copy-done((bf16[16,4,384,384]{3,2,1,0:T(8,128)(2,1)S(1)}, bf16[16,4,384,384]{3,2,1,0:T(8,128)(2,1)}, u32[]{:S(2)}) %copy-start) | copy-done | bytes 18874392
  8.2 0.0 copy-start.1
  8.2 1.9 %copy-done.1 = bf16[16,384,256]{2,1,0:T(8,128)(2,1)S(1)} copy-done((bf16[16,384,256]{2,1,0:T(8,128)(2,1)S(1)}, bf16[16,384,256]{2,1,0:T(8,128)(2,1)}, u32[]{:S(2)}) %copy-start.1) | copy-done | bytes 3145752
  10.1 0.0 slice-start
  10.1 0.0 slice-start.1
  10.1 0.0 slice-start.2
  10.1 5.1 %shard_map.59 = bf16[4,384,256]{2,1,0:T(8,128)(2,1)} custom-call(s32[4]{0:T(128)S(1)} %get-tuple-element.7.order_ref, f32[64]{0:T(128)S(1)} %reshape.35.mpo_ref, bf16[16,4,384,384]{3,2,1,0:T(8,128)(2,1)S(1)} %copy-done, bf16[16,384,256]{2,1,0:T(8,128)(2,1)S(1)} %copy-done.1), custom_call_target="tpu_custom_call" | custom-call | flops 2013265920 | bytes 7077888 | tf_op jit(solution)/shard_map/pallas_call | solution.py:67
  15.2 0.0 collective-permute-start.3
  15.2 0.1 fusion.2
  15.2 0.0 slice-start.3
  15.2 0.0 slice-start.4
  15.2 3.2 %shard_map.57 = bf16[2,384,256]{2,1,0:T(8,128)(2,1)} custom-call(s32[2]{0:T(128)S(1)} %get-tuple-element.9.order_ref, f32[64]{0:T(128)S(1)} %reshape.35.mpo_ref, bf16[16,4,384,384]{3,2,1,0:T(8,128)(2,1)S(1)} %copy-done, bf16[16,384,256]{2,1,0:T(8,128)(2,1)S(1)} %copy-done.1), custom_call_target="tpu_custom_call" | custom-call | flops 1006632960 | bytes 3538944 | tf_op jit(solution)/shard_map/pallas_call | solution.py:67
  18.5 0.5 collective-permute-start.1
  19.0 0.0 slice-done
  19.0 0.0 slice-done.1
  19.0 0.0 slice-done.2
  19.0 0.0 slice-done.3
  19.0 0.0 slice-done.4
  19.0 0.0 slice-start.5
  19.0 0.0 slice-start.6
  19.0 0.0 slice-start.7
  19.0 3.2 %shard_map.55 = bf16[2,384,256]{2,1,0:T(8,128)(2,1)} custom-call(s32[2]{0:T(128)S(1)} %get-tuple-element.11.order_ref, f32[64]{0:T(128)S(1)} %reshape.35.mpo_ref, bf16[16,4,384,384]{3,2,1,0:T(8,128)(2,1)S(1)} %bitcast.18, bf16[16,384,256]{2,1,0:T(8,128)(2,1)S(1)} %copy-done.1), custom_call_target="tpu_custom_call" | custom-call | flops 1006632960 | bytes 3538944 | tf_op jit(solution)/shard_map/pallas_call | solution.py:67
  22.3 0.0 collective-permute-start
  22.3 0.0 collective-permute-done.1.rest_0_
  22.3 0.0 copy-start.2
  22.3 0.8 copy-done.2
  23.0 0.0 copy-start.3
  23.0 1.0 %copy-done.3 = bf16[2,384,256]{2,1,0:T(8,128)(2,1)S(1)} copy-done((bf16[2,384,256]{2,1,0:T(8,128)(2,1)S(1)}, bf16[2,384,256]{2,1,0:T(8,128)(2,1)}, u32[]{:S(2)}) %copy-start.3) | copy-done | bytes 393240
  24.0 0.0 slice-start.8
  24.0 0.0 slice-start.9
  24.0 3.2 %shard_map.58 = bf16[2,384,256]{2,1,0:T(8,128)(2,1)} custom-call(s32[2]{0:T(128)S(1)} %get-tuple-element.10.order_ref, f32[64]{0:T(128)S(1)} %reshape.35.mpo_ref, bf16[16,4,384,384]{3,2,1,0:T(8,128)(2,1)S(1)} %bitcast.18, bf16[16,384,256]{2,1,0:T(8,128)(2,1)S(1)} %copy-done.1, bf16[2,384,256]{2,1,0:T(8,128)(2,1)S(1)} %copy-done.3), custom_call_target="tpu_custom_call" | custom-call | flops 1006632960 | bytes 3538944 | tf_op jit(solution)/shard_map/pallas_call | solution.py:67
  27.3 4.0 %collective-permute-start.2 = (bf16[2,384,256]{2,1,0:T(8,128)(2,1)}, bf16[2,384,256]{2,1,0:T(8,128)(2,1)S(1)}, u32[]{:S(2)}, u32[]{:S(2)}) collective-permute-start(bf16[2,384,256]{2,1,0:T(8,128)(2,1)} %shard_map.58), channel_id=1, source_target_pairs={{0,64},{16,80},{32,96},{48,112},{64,0},{80,16},{96,32},{112,48},{1... | collective-permute-start | bytes 1179656 | tf_op jit(solution)/shard_map/ppermute | solution.py:200
  31.2 0.0 collective-permute-done.3.rest_0_
  31.2 0.0 slice-done.5
  31.2 0.0 slice-done.6
  31.2 0.0 slice-done.7
  31.3 0.0 slice-done.8
  31.3 0.0 slice-done.9
  31.3 5.4 %shard_map.60 = bf16[4,384,256]{2,1,0:T(8,128)(2,1)S(1)} custom-call(s32[4]{0:T(128)S(1)} %get-tuple-element.8.order_ref, f32[64]{0:T(128)S(1)} %reshape.35.mpo_ref, bf16[16,4,384,384]{3,2,1,0:T(8,128)(2,1)S(1)} %bitcast.20, bf16[16,384,256]{2,1,0:T(8,128)(2,1)S(1)} %copy-done.1, bf16[4,384,256]{2,1,0:T(8,128)(2,1)} %collective-permute-done.3.rest_0_), custom_call_target="tpu_custom_call" | custom-call | flops 2013265920 | bytes 7077888 | tf_op jit(solution)/shard_map/pallas_call | solution.py:67
  36.7 0.1 fusion
  36.7 1.1 %collective-permute-start.4 = (bf16[2,384,256]{2,1,0:T(8,128)(2,1)S(1)}, bf16[2,384,256]{2,1,0:T(8,128)(2,1)S(1)}, u32[]{:S(2)}, u32[]{:S(2)}) collective-permute-start(bf16[2,384,256]{2,1,0:T(8,128)(2,1)S(1)} %get-tuple-element.6), channel_id=1, source_target_pairs={{0,32},{16,48},{32,64},{48,80},{64,96},{80,112},{96,0},{112,16},{1... | collective-permute-start | bytes 1179656 | tf_op jit(solution)/shard_map/ppermute | solution.py:202
  37.8 2.2 %collective-permute-start.5 = (bf16[2,384,256]{2,1,0:T(8,128)(2,1)S(1)}, bf16[2,384,256]{2,1,0:T(8,128)(2,1)S(1)}, u32[]{:S(2)}, u32[]{:S(2)}) collective-permute-start(bf16[2,384,256]{2,1,0:T(8,128)(2,1)S(1)} %get-tuple-element.5), channel_id=1, source_target_pairs={{0,96},{16,112},{32,0},{48,16},{64,32},{80,48},{96,64},{112,80},{1... | collective-permute-start | bytes 1179656 | tf_op jit(solution)/shard_map/ppermute | solution.py:203
  40.0 0.0 collective-permute-done.rest_0_
  40.0 0.0 copy-start.4
  40.0 3.5 %shard_map.56.own_ref = f32[2,384,256]{2,1,0:T(8,128)S(1)} custom-call(s32[2]{0:T(128)S(1)} %get-tuple-element.12.order_ref, f32[64]{0:T(128)S(1)} %reshape.35.mpo_ref, bf16[16,4,384,384]{3,2,1,0:T(8,128)(2,1)S(1)} %bitcast.20, bf16[16,384,256]{2,1,0:T(8,128)(2,1)S(1)} %copy-done.1, bf16[2,384,256]{2,1,0:T(8,128)(2,1)} %collective-permute-done.rest_0_), custom_call_target="tpu_custom_call" | custom-call | flops 1006632960 | bytes 3538944 | tf_op jit(solution)/shard_map/pallas_call | solution.py:67
  43.5 0.0 collective-permute-done.2.far_ref
  43.5 6.1 %collective-permute-done.4.up_ref = bf16[2,384,256]{2,1,0:T(8,128)(2,1)S(1)} collective-permute-done((bf16[2,384,256]{2,1,0:T(8,128)(2,1)S(1)}, bf16[2,384,256]{2,1,0:T(8,128)(2,1)S(1)}, u32[]{:S(2)}, u32[]{:S(2)}) %collective-permute-start.4) | collective-permute-done | bytes 393248 | tf_op jit(solution)/shard_map/ppermute | solution.py:202
  49.6 0.7 collective-permute-done.5.down_ref
  50.4 5.7 %shard_map.61 = bf16[8,2,48,256]{3,2,1,0:T(8,128)(2,1)S(1)} custom-call(f32[2,384,256]{2,1,0:T(8,128)S(1)} %shard_map.56.own_ref, bf16[2,384,256]{2,1,0:T(8,128)(2,1)S(1)} %collective-permute-done.2.far_ref, bf16[2,384,256]{2,1,0:T(8,128)(2,1)S(1)} %collective-permute-done.4.up_ref, bf16[2,384,256]{2,1,0:T(8,128)(2,1)S(1)} %collective-permute-done.5.down_ref), custom_call_target="tpu_custom_call" | custom-call | flops 3623878656 | bytes 2359296 | tf_op jit(solution)/shard_map/pallas_call | solution.py:148
  56.1 12.8 %all_to_all.10 = bf16[8,2,48,256]{3,2,1,0:T(8,128)(2,1)} all-to-all(bf16[8,2,48,256]{3,2,1,0:T(8,128)(2,1)S(1)} %shard_map.61), channel_id=1, replica_groups=mesh['mpo'=8,'sec'=16] {'mpo'}, dimensions={0} | all-to-all | bytes 786432 | tf_op jit(solution)/shard_map/all_to_all | solution.py:207
  68.8 7.0 %all-to-all-start.1 = ((bf16[16,48,256]{2,1,0:T(8,128)(2,1)}), bf16[16,48,256]{2,1,0:T(8,128)(2,1)S(1)}, u32[]{:S(2)}, u32[]{:S(2)}) async-start(bf16[16,48,256]{2,1,0:T(8,128)(2,1)} %bitcast.16), calls=%async_computation.1 | async-start | bytes 786432 | tf_op jit(solution)/shard_map/all_to_all | solution.py:209
  75.9 0.0 copy-done.4
  75.9 0.1 iota_compare_fusion
  76.0 9.5 %all-to-all-done.1 = bf16[16,48,256]{2,1,0:T(8,128)(2,1)S(1)} async-done(((bf16[16,48,256]{2,1,0:T(8,128)(2,1)}), bf16[16,48,256]{2,1,0:T(8,128)(2,1)S(1)}, u32[]{:S(2)}, u32[]{:S(2)}) %all-to-all-start.1) | async-done | bytes 393248 | tf_op jit(solution)/shard_map/all_to_all | solution.py:209
  85.5 0.8 broadcast_select_fusion
  (2 shorter events, 0.0 us)
Async XLA Ops:
  1.8 6.4 %copy-start = (bf16[16,4,384,384]{3,2,1,0:T(8,128)(2,1)S(1)}, bf16[16,4,384,384]{3,2,1,0:T(8,128)(2,1)}, u32[]{:S(2)}) copy-start(bf16[16,4,384,384]{3,2,1,0:T(8,128)(2,1)} %left_ref.11) | copy-start | bytes 56623108
  8.2 1.9 %copy-start.1 = (bf16[16,384,256]{2,1,0:T(8,128)(2,1)S(1)}, bf16[16,384,256]{2,1,0:T(8,128)(2,1)}, u32[]{:S(2)}) copy-start(bf16[16,384,256]{2,1,0:T(8,128)(2,1)} %site_ref.11) | copy-start | bytes 9437188
  10.1 8.9 %slice-start = ((s8[18874368]{0:T(1024)(128)(4,1)}), s8[4194304]{0:T(1024)(128)(4,1)S(1)}, s32[]{:S(2)}) async-start(s8[18874368]{0:T(1024)(128)(4,1)} %bitcast.17), calls=%async_computation.2 | async-start | bytes 8388608
  10.1 8.9 %slice-start.1 = ((s8[18874368]{0:T(1024)(128)(4,1)}), s8[4194304]{0:T(1024)(128)(4,1)S(1)}, s32[]{:S(2)}) async-start(s8[18874368]{0:T(1024)(128)(4,1)} %bitcast.17), calls=%async_computation.3 | async-start | bytes 8388608
  10.1 8.9 %slice-start.2 = ((s8[18874368]{0:T(1024)(128)(4,1)}), s8[4194304]{0:T(1024)(128)(4,1)S(1)}, s32[]{:S(2)}) async-start(s8[18874368]{0:T(1024)(128)(4,1)} %bitcast.17), calls=%async_computation.4 | async-start | bytes 8388608
  15.2 16.1 %collective-permute-start.3 = (bf16[4,384,256]{2,1,0:T(8,128)(2,1)}, bf16[4,384,256]{2,1,0:T(8,128)(2,1)}, u32[]{:S(2)}, u32[]{:S(2)}) collective-permute-start(bf16[4,384,256]{2,1,0:T(8,128)(2,1)} %shard_map.59), channel_id=1, source_target_pairs={{0,16},{16,0},{32,48},{48,32},{64,80},{80,64},{96,112},{112,96},{1... | collective-permute-start | bytes 2359304 | tf_op jit(solution)/shard_map/ppermute | solution.py:199
  15.2 3.8 %slice-start.3 = ((s8[18874368]{0:T(1024)(128)(4,1)}), s8[4194304]{0:T(1024)(128)(4,1)S(1)}, s32[]{:S(2)}) async-start(s8[18874368]{0:T(1024)(128)(4,1)} %bitcast.17), calls=%async_computation.5 | async-start | bytes 8388608
  15.2 3.8 %slice-start.4 = ((s8[18874368]{0:T(1024)(128)(4,1)}), s8[2097152]{0:T(1024)(128)(4,1)S(1)}, s32[]{:S(2)}) async-start(s8[18874368]{0:T(1024)(128)(4,1)} %bitcast.17), calls=%async_computation.6 | async-start | bytes 4194304
  18.5 3.8 %collective-permute-start.1 = (bf16[2,384,256]{2,1,0:T(8,128)(2,1)}, bf16[2,384,256]{2,1,0:T(8,128)(2,1)S(1)}, u32[]{:S(2)}, u32[]{:S(2)}) collective-permute-start(bf16[2,384,256]{2,1,0:T(8,128)(2,1)} %shard_map.57), channel_id=1, source_target_pairs={{0,16},{16,0},{32,48},{48,32},{64,80},{80,64},{96,112},{112,96},{1... | collective-permute-start | bytes 1179656 | tf_op jit(solution)/shard_map/ppermute | solution.py:198
  19.0 12.2 %slice-start.5 = ((s8[18874368]{0:T(1024)(128)(4,1)}), s8[2097152]{0:T(1024)(128)(4,1)S(1)}, s32[]{:S(2)}) async-start(s8[18874368]{0:T(1024)(128)(4,1)} %bitcast.19), calls=%async_computation.7 | async-start | bytes 4194304
  19.0 12.2 %slice-start.6 = ((s8[18874368]{0:T(1024)(128)(4,1)}), s8[4194304]{0:T(1024)(128)(4,1)S(1)}, s32[]{:S(2)}) async-start(s8[18874368]{0:T(1024)(128)(4,1)} %bitcast.19), calls=%async_computation.8 | async-start | bytes 8388608
  19.0 12.2 %slice-start.7 = ((s8[18874368]{0:T(1024)(128)(4,1)}), s8[4194304]{0:T(1024)(128)(4,1)S(1)}, s32[]{:S(2)}) async-start(s8[18874368]{0:T(1024)(128)(4,1)} %bitcast.19), calls=%async_computation.9 | async-start | bytes 8388608
  22.3 17.8 %collective-permute-start = (bf16[2,384,256]{2,1,0:T(8,128)(2,1)}, bf16[2,384,256]{2,1,0:T(8,128)(2,1)}, u32[]{:S(2)}, u32[]{:S(2)}) collective-permute-start(bf16[2,384,256]{2,1,0:T(8,128)(2,1)} %shard_map.55), channel_id=1, source_target_pairs={{0,16},{16,0},{32,48},{48,32},{64,80},{80,64},{96,112},{112,96},{1... | collective-permute-start | bytes 1179656 | tf_op jit(solution)/shard_map/ppermute | solution.py:204
  22.3 0.8 copy-start.2
  23.0 1.0 %copy-start.3 = (bf16[2,384,256]{2,1,0:T(8,128)(2,1)S(1)}, bf16[2,384,256]{2,1,0:T(8,128)(2,1)}, u32[]{:S(2)}) copy-start(bf16[2,384,256]{2,1,0:T(8,128)(2,1)} %copy-done.2) | copy-start | bytes 1179652
  24.0 7.2 %slice-start.8 = ((s8[18874368]{0:T(1024)(128)(4,1)}), s8[4194304]{0:T(1024)(128)(4,1)S(1)}, s32[]{:S(2)}) async-start(s8[18874368]{0:T(1024)(128)(4,1)} %bitcast.19), calls=%async_computation.10 | async-start | bytes 8388608
  24.0 7.2 %slice-start.9 = ((s8[18874368]{0:T(1024)(128)(4,1)}), s8[4194304]{0:T(1024)(128)(4,1)S(1)}, s32[]{:S(2)}) async-start(s8[18874368]{0:T(1024)(128)(4,1)} %bitcast.19), calls=%async_computation.11 | async-start | bytes 8388608
  27.3 16.2 %collective-permute-start.2 = (bf16[2,384,256]{2,1,0:T(8,128)(2,1)}, bf16[2,384,256]{2,1,0:T(8,128)(2,1)S(1)}, u32[]{:S(2)}, u32[]{:S(2)}) collective-permute-start(bf16[2,384,256]{2,1,0:T(8,128)(2,1)} %shard_map.58), channel_id=1, source_target_pairs={{0,64},{16,80},{32,96},{48,112},{64,0},{80,16},{96,32},{112,48},{1... | collective-permute-start | bytes 1179656 | tf_op jit(solution)/shard_map/ppermute | solution.py:200
  36.7 12.9 %collective-permute-start.4 = (bf16[2,384,256]{2,1,0:T(8,128)(2,1)S(1)}, bf16[2,384,256]{2,1,0:T(8,128)(2,1)S(1)}, u32[]{:S(2)}, u32[]{:S(2)}) collective-permute-start(bf16[2,384,256]{2,1,0:T(8,128)(2,1)S(1)} %get-tuple-element.6), channel_id=1, source_target_pairs={{0,32},{16,48},{32,64},{48,80},{64,96},{80,112},{96,0},{112,16},{1... | collective-permute-start | bytes 1179656 | tf_op jit(solution)/shard_map/ppermute | solution.py:202
  37.8 12.6 %collective-permute-start.5 = (bf16[2,384,256]{2,1,0:T(8,128)(2,1)S(1)}, bf16[2,384,256]{2,1,0:T(8,128)(2,1)S(1)}, u32[]{:S(2)}, u32[]{:S(2)}) collective-permute-start(bf16[2,384,256]{2,1,0:T(8,128)(2,1)S(1)} %get-tuple-element.5), channel_id=1, source_target_pairs={{0,96},{16,112},{32,0},{48,16},{64,32},{80,48},{96,64},{112,80},{1... | collective-permute-start | bytes 1179656 | tf_op jit(solution)/shard_map/ppermute | solution.py:203
  40.0 35.9 %copy-start.4 = (s32[16]{0:T(128)S(1)}, s32[16]{0:T(128)}, u32[]{:S(2)}) copy-start(s32[16]{0:T(128)} %param.9) | copy-start | bytes 196
  68.8 16.7 %all-to-all-start.1 = ((bf16[16,48,256]{2,1,0:T(8,128)(2,1)}), bf16[16,48,256]{2,1,0:T(8,128)(2,1)S(1)}, u32[]{:S(2)}, u32[]{:S(2)}) async-start(bf16[16,48,256]{2,1,0:T(8,128)(2,1)} %bitcast.16), calls=%async_computation.1 | async-start | bytes 786432 | tf_op jit(solution)/shard_map/all_to_all | solution.py:209

commit v2 on v1

v2 whole, which is shorter than its diff:
```python
import functools

import jax
import jax.numpy as jnp
from jax import lax
from jax.experimental import pallas as pl
from jax.experimental.pallas import tpu as pltpu
from jax.sharding import PartitionSpec as P

ITERS = 6
EARLY = 4
PHYS = 4
CHIPS = 4
TERM_MIB = 57
F32, BF16 = jnp.float32, jnp.bfloat16


def mixing_matrix(mpo_ref, out_ref, wslices, phys, right):
    per = 128 // right
    row = lax.broadcasted_iota(jnp.int32, (right, 128), 0)
    lane = lax.broadcasted_iota(jnp.int32, (right, 128), 1)
    for s in range(phys):
        for w in range(wslices):
            for t in range(0, phys, per):
                block = jnp.zeros((right, 128), F32)
                for p in range(per):
                    value = mpo_ref[(w * phys + s) * phys + t + p]
                    block = jnp.where(lane == row + p * right, value, block)
                column = (w * phys + t) * right
                out_ref[s * right : (s + 1) * right, column : column + 128] = block.astype(BF16)


def mix(site, mix_ref, stacked_ref):
    rows, columns = site.shape
    for w in range(stacked_ref.shape[0] // rows):
        stacked_ref[w * rows : (w + 1) * rows] = jnp.dot(
            site, mix_ref[:, w * columns : (w + 1) * columns], preferred_element_type=F32
        ).astype(BF16)


def contract(left_ref, stacked_ref):
    left = jnp.concatenate([left_ref[w] for w in range(left_ref.shape[0])], axis=1)
    return jnp.dot(left, stacked_ref[...], preferred_element_type=F32)


def term_kernel(me_ref, slot_ref, mpo_ref, left_hbm, site_hbm, *rest, groups):
    added = sum(offset is not None for _, _, offset in groups)
    others, outs = list(rest[:added]), rest[added : added + len(groups)]
    left_ref, site_ref, mix_ref, stacked_ref, inverse_ref, left_sem, site_sem = rest[
        added + len(groups) :
    ]
    wslices = left_ref.shape[1]
    columns = site_ref.shape[2]
    chip, core = lax.div(me_ref[0], 2), lax.rem(me_ref[0], 2)
    for k in range(slot_ref.shape[0]):
        inverse_ref[slot_ref[k]] = k
    work = []
    for g, (targets, _, offset) in enumerate(groups):
        other = None if offset is None else others.pop(0)
        for j, (step, flip) in enumerate(targets):
            member = 2 * lax.rem(chip + step, CHIPS) + (1 - core if flip else core)
            copies = []
            for b in range(2):
                n = 2 * len(work) + b
                sector = inverse_ref[2 * member + b]
                copies.append(
                    pltpu.make_async_copy(site_hbm.at[sector], site_ref.at[n], site_sem.at[n])
                )
                copies.append(
                    pltpu.make_async_copy(left_hbm.at[sector], left_ref.at[n], left_sem.at[n])
                )
            for copy in copies:
                copy.start()
            work.append((copies, outs[g], other, offset, 2 * j))
    mixing_matrix(mpo_ref, mix_ref, wslices, PHYS, columns // PHYS)
    for i, (copies, out_ref, other_ref, offset, start) in enumerate(work):
        for copy in copies:
            copy.wait()
        for b in range(2):
            mix(site_ref[2 * i + b], mix_ref, stacked_ref.at[b])
        for b in range(2):
            term = contract(left_ref.at[2 * i + b], stacked_ref.at[b])
            if other_ref is not None:
                term = term + other_ref[offset + start + b].astype(F32)
            out_ref[start + b] = term.astype(out_ref.dtype)


def terms(me, slots, mpo_flat, left_env, site, *groups):
    sectors, wslices, rows, _ = left_env.shape
    columns = site.shape[2]
    count = 2 * sum(len(targets) for targets, _, _ in groups)
    vmem = pl.BlockSpec(memory_space=pltpu.VMEM)
    smem = pl.BlockSpec(memory_space=pltpu.SMEM)
    hbm = pl.BlockSpec(memory_space=pltpu.HBM)
    others = [other[0] for _, _, other in groups if other is not None]
    flops = 2 * count * rows * columns * wslices * (rows + columns)
    moved = count * (wslices * rows * rows * 2 + rows * columns * 2)
    return pl.pallas_call(
        functools.partial(
            term_kernel,
            groups=[(targets, dtype, other and other[1]) for targets, dtype, other in groups],
        ),
        out_shape=[
            jax.ShapeDtypeStruct((2 * len(targets), rows, columns), dtype)
            for targets, dtype, _ in groups
        ],
        in_specs=[smem, smem, smem, hbm, hbm] + [vmem] * len(others),
        out_specs=[vmem] * len(groups),
        scratch_shapes=[
            pltpu.VMEM((count, wslices, rows, rows), BF16),
            pltpu.VMEM((count, rows, columns), BF16),
            pltpu.VMEM((columns, wslices * columns), BF16),
            pltpu.VMEM((2, wslices * rows, columns), BF16),
            pltpu.SMEM((sectors,), jnp.int32),
            pltpu.SemaphoreType.DMA((count,)),
            pltpu.SemaphoreType.DMA((count,)),
        ],
        compiler_params=pltpu.CompilerParams(vmem_limit_bytes=TERM_MIB * 2**20),
        cost_estimate=pl.CostEstimate(flops=flops, bytes_accessed=moved, transcendentals=0),
    )(me, slots, mpo_flat, left_env, site, *others)


def split(a):
    high = a.astype(BF16)
    return high, (a - high.astype(F32)).astype(BF16)


def product(a, b):
    return jnp.dot(
        jnp.concatenate([a[0], a[0], a[1]], axis=1),
        jnp.concatenate([b[0], b[1], b[0]], axis=0),
        preferred_element_type=F32,
    )


def root_kernel(own_ref, other_ref, far_ref, up_ref, down_ref, out_ref):
    count, rows, columns = far_ref.shape
    parts, _, part_rows, _ = out_ref.shape
    eye = lax.broadcasted_iota(jnp.int32, (columns, columns), 0) == lax.broadcasted_iota(
        jnp.int32, (columns, columns), 1
    )
    identity = eye.astype(F32)
    sectors = range(count)
    term, current, scale = [], [], []
    for b in sectors:
        total = (
            own_ref[b]
            + other_ref[b].astype(F32)
            + far_ref[b].astype(F32)
            + up_ref[b].astype(F32)
            + down_ref[b].astype(F32)
        )
        high, low = split(total)
        gram = lax.dot_general(
            jnp.concatenate([high, high, low], axis=0),
            jnp.concatenate([high, low, high], axis=0),
            (((0,), (0,)), ((), ())),
            preferred_element_type=F32,
        )
        norm = jnp.sqrt(jnp.sum(gram * gram, keepdims=True))
        term.append((high, low))
        current.append(gram / norm)
        scale.append(1.0 / jnp.sqrt(norm))
    partner = [None] * count
    for repeat in range(ITERS):
        if repeat < EARLY:
            rounded = [current[b].astype(BF16) for b in sectors]
            if repeat == 0:
                step = current
            else:
                others = [partner[b].astype(BF16) for b in sectors]
                step = [
                    jnp.dot(others[b], rounded[b], preferred_element_type=F32) for b in sectors
                ]
            small = [step[b].astype(BF16) for b in sectors]
            current = [
                1.5 * current[b]
                - 0.5 * jnp.dot(rounded[b], small[b], preferred_element_type=F32)
                for b in sectors
            ]
            if repeat == 0:
                partner = [1.5 * identity - 0.5 * step[b] for b in sectors]
            else:
                partner = [
                    1.5 * partner[b]
                    - 0.5 * jnp.dot(small[b], others[b], preferred_element_type=F32)
                    for b in sectors
                ]
        else:
            halves = [split(current[b]) for b in sectors]
            others = [split(partner[b]) for b in sectors]
            factor = [1.5 * identity - 0.5 * product(others[b], halves[b]) for b in sectors]
            pairs = [split(factor[b]) for b in sectors]
            if repeat < ITERS - 1:
                current = [product(halves[b], pairs[b]) for b in sectors]
            partner = [product(pairs[b], others[b]) for b in sectors]
    for b in sectors:
        result = (product(term[b], split(partner[b] * scale[b]))).astype(BF16)
        for m in range(parts):
            out_ref[m, b] = result[m * part_rows : (m + 1) * part_rows]


def expansions(own, other, far, up, down, parts):
    count, rows, columns = far.shape
    flops = 2 * 3 * count * columns * columns * (15 * columns + 2 * rows)
    return pl.pallas_call(
        root_kernel,
        out_shape=jax.ShapeDtypeStruct((parts, count, rows // parts, columns), BF16),
        in_specs=[pl.BlockSpec(memory_space=pltpu.VMEM)] * 5,
        out_specs=pl.BlockSpec(memory_space=pltpu.VMEM),
        compiler_params=pltpu.CompilerParams(vmem_limit_bytes=40 * 2**20),
        cost_estimate=pl.CostEstimate(
            flops=flops, bytes_accessed=count * rows * columns * 12, transcendentals=0
        ),
    )(own, other, far, up, down)


def shards(left_env, site_tensor, mpo_column, sector_slot, kept):
    columns = site_tensor.shape[2]
    members = lax.axis_size("mpo")
    me = lax.axis_index("mpo").reshape(1)
    swap = [(2 * c + q, 2 * c + 1 - q) for c in range(CHIPS) for q in range(2)]

    def shift(step):
        return [
            (2 * c + q, 2 * ((c + step) % CHIPS) + q) for c in range(CHIPS) for q in range(2)
        ]

    flat = mpo_column.astype(F32).reshape(-1)
    after = lax.optimization_barrier

    def run(slots, *groups):
        return terms(me, slots, flat, left_env, site_tensor, *groups)

    far_other, near_other, far_own = run(
        sector_slot,
        ([(2, 1)], BF16, None),
        ([(1, 1), (3, 1)], BF16, None),
        ([(2, 0)], F32, None),
    )
    far_other = lax.ppermute(far_other, "mpo", swap)
    near_other, far_other = after((near_other, far_other))
    near_other = lax.ppermute(near_other, "mpo", swap)
    far = (far_own + far_other.astype(F32)).astype(BF16)
    far = lax.ppermute(far, "mpo", shift(2))
    up, down, own_other = run(
        sector_slot,
        ([(1, 0)], BF16, (near_other, 0)),
        ([(3, 0)], BF16, (near_other, 2)),
        ([(0, 1)], BF16, None),
    )
    up, slots = after((up, sector_slot))
    up = lax.ppermute(up, "mpo", shift(1))
    down = lax.ppermute(down, "mpo", shift(3))
    own_other = lax.ppermute(own_other, "mpo", swap)
    (own,) = run(slots, ([(0, 0)], F32, None))
    result = expansions(own, own_other, far, up, down, members)
    rows = lax.all_to_all(result, "mpo", split_axis=0, concat_axis=0, tiled=True)
    rows = rows.reshape(-1, rows.shape[2], columns)
    routed = lax.all_to_all(rows, "sec", split_axis=0, concat_axis=0, tiled=True)
    keep = jnp.arange(columns, dtype=jnp.int32)[None, None, :] < kept[:, None, None]
    return jnp.where(keep, routed, jnp.zeros((), BF16))


def solution(mesh):
    return jax.shard_map(
        shards,
        mesh=mesh,
        in_specs=(
            P("sec", "mpo", None, None),
            P("sec", None, None),
            P("mpo", None, None),
            P("sec"),
            P("sec"),
        ),
        out_specs=P("sec", "mpo", None),
        check_vma=False,
    )
```

time: 86.7 us -> 75.3 us (0.87)
  local copies, waits for them, and re-layouts: 11.1 us -> 3.4 us
  Pallas kernels: 29.3 us -> 24.8 us
    unnamed x30 -> x6, local copies, waits for them, and re-layouts: 10 us -> 2.02 us
    pallas_call x6 -> x3, Pallas kernels: 23.6 us -> 20.6 us  [terms(): pl.pallas_call(functools.partial(term_kernel, groups=[(targets, dtype, ot...]
    pallas_call x1, Pallas kernels: 5.66 us -> 4.25 us  [expansions(): pl.pallas_call(root_kernel, out_shape=jax.ShapeDtypeStruct((parts, count,...]
    convert_element_type x0 -> x1, other arithmetic: none -> 1.22 us  [shards(): far = (far_own + far_other.astype(F32)).astype(BF16)]
  transfers between devices with their start and end apart: 7 -> 7, of which waited for: 3 -> 4; matrix products, arithmetic and copies ran while one was open for 0% -> 2% of each run, Pallas kernels for 21% -> 16%
where the time goes in v2:
time: 75.3 us; the launch traced here: 74.9 us
  Pallas kernels  24.8 us (33%)
  waiting for transfers between devices  16.4 us (22%)
  starting transfers between devices  14.6 us (19%)
  blocking collectives  13.6 us (18%)
  local copies, waits for them, and re-layouts  3.4 us (5%)
  other arithmetic  2.07 us (3%)
    pallas_call x3, Pallas kernels, terms(): pl.pallas_call(functools.partial(term_kernel, groups=[(targets, dtype, ot...  20.6 us
    all_to_all x1, blocking collectives, shards(): lax.all_to_all(result, 'mpo', split_axis=0, concat_axis=0, tiled=True)  13.6 us
    all_to_all x1, waiting for transfers between devices, shards(): lax.all_to_all(rows, 'sec', split_axis=0, concat_axis=0, tiled=True)  9.54 us
    all_to_all x1, starting transfers between devices, shards(): lax.all_to_all(rows, 'sec', split_axis=0, concat_axis=0, tiled=True)  7.03 us
    ppermute x1, waiting for transfers between devices, shards(): up = lax.ppermute(up, 'mpo', shift(1))  4.66 us
    pallas_call x1, Pallas kernels, expansions(): pl.pallas_call(root_kernel, out_shape=jax.ShapeDtypeStruct((parts, count,...  4.25 us
    ppermute x1, starting transfers between devices, shards(): far = lax.ppermute(far, 'mpo', shift(2))  4.05 us
    ppermute x1, starting transfers between devices, shards(): down = lax.ppermute(down, 'mpo', shift(3))  2.22 us
  transfers between devices with their start and end apart: 7, of which 4 were waited for; matrix products, arithmetic and copies ran while one was open for 2% of the time, Pallas kernels for 16%

profile of v2, /device:TPU:0, one launch (start us, length us, event | category | flops | bytes accessed | tf_op | source)
XLA Modules:
  0.0 74.9 jit_solution(2384208572803054531)
XLA Ops:
  0.0 1.4 %reshape.37.mpo_ref = f32[64]{0:T(128)} reshape(bf16[4,4,4]{2,1,0:T(4,128)(2,1)} %param.7) | data formatting | bytes 384 | tf_op jit(solution)/shard_map/reshape | solution.py:229
  1.4 8.3 %shard_map.55 = (bf16[2,384,256]{2,1,0:T(8,128)(2,1)}, bf16[4,384,256]{2,1,0:T(8,128)(2,1)}, f32[2,384,256]{2,1,0:T(8,128)}) custom-call(s32[1]{0:T(128)} %bitcast.me_ref, s32[16]{0:T(128)} %slot_ref.4, f32[64]{0:T(128)} %reshape.37.mpo_ref, bf16[16,4,384,384]{3,2,1,0:T(8,128)(2,1)} %left_hbm.5, bf16[16,384,256]{2,1,0:T(8,128)(2,1)} %site_hbm.5), custom_call_target="tpu_custom_call" | custom-call | flops 4026531840 | bytes 11010048 | tf_op jit(solution)/shard_map/pallas_call | solution.py:98
  9.7 0.1 collective-permute-start
  9.8 1.9 %collective-permute-done = bf16[2,384,256]{2,1,0:T(8,128)(2,1)S(1)} collective-permute-done((bf16[2,384,256]{2,1,0:T(8,128)(2,1)}, bf16[2,384,256]{2,1,0:T(8,128)(2,1)S(1)}, u32[]{:S(2)}, u32[]{:S(2)}) %collective-permute-start) | collective-permute-done | bytes 393248 | tf_op jit(solution)/shard_map/ppermute | solution.py:241
  11.7 0.1 collective-permute-start.1
  11.8 1.2 %add_convert_fusion = bf16[2,384,256]{2,1,0:T(8,128)(2,1)S(1)} fusion(f32[2,384,256]{2,1,0:T(8,128)} %get-tuple-element.21, bf16[2,384,256]{2,1,0:T(8,128)(2,1)S(1)} %collective-permute-done), kind=kLoop, calls=%fused_computation | loop fusion | flops 589824 | bytes 1572864 | tf_op jit(solution)/shard_map/convert_element_type | solution.py:244
  13.1 4.1 %collective-permute-start.3 = (bf16[2,384,256]{2,1,0:T(8,128)(2,1)S(1)}, bf16[2,384,256]{2,1,0:T(8,128)(2,1)S(1)}, u32[]{:S(2)}, u32[]{:S(2)}) collective-permute-start(bf16[2,384,256]{2,1,0:T(8,128)(2,1)S(1)} %add_convert_fusion), channel_id=1, source_target_pairs={{0,64},{16,80},{32,96},{48,112},{64,0},{80,16},{96,32},{112,48},{1... | collective-permute-start | bytes 1179656 | tf_op jit(solution)/shard_map/ppermute | solution.py:245
  17.1 0.0 collective-permute-done.1.rest_0_.rest_1_
  17.1 0.0 copy-start.1
  17.1 0.9 %copy-done.1 = bf16[4,384,256]{2,1,0:T(8,128)(2,1)} copy-done((bf16[4,384,256]{2,1,0:T(8,128)(2,1)}, bf16[4,384,256]{2,1,0:T(8,128)(2,1)S(1)}, u32[]{:S(2)}) %copy-start.1) | copy-done | bytes 786456
  18.0 7.7 %shard_map.56 = (bf16[2,384,256]{2,1,0:T(8,128)(2,1)}, bf16[2,384,256]{2,1,0:T(8,128)(2,1)}, bf16[2,384,256]{2,1,0:T(8,128)(2,1)}) custom-call(s32[1]{0:T(128)} %bitcast.me_ref, s32[16]{0:T(128)} %slot_ref.4, f32[64]{0:T(128)} %reshape.37.mpo_ref, bf16[16,4,384,384]{3,2,1,0:T(8,128)(2,1)} %left_hbm.5, bf16[16,384,256]{2,1,0:T(8,128)(2,1)} %site_hbm.5, ...), custom_call_target="tpu_custom_call" | custom-call | flops 3019898880 | bytes 8257536 | tf_op jit(solution)/shard_map/pallas_call | solution.py:98
  25.7 1.1 %collective-permute-start.4 = (bf16[2,384,256]{2,1,0:T(8,128)(2,1)}, bf16[2,384,256]{2,1,0:T(8,128)(2,1)S(1)}, u32[]{:S(2)}, u32[]{:S(2)}) collective-permute-start(bf16[2,384,256]{2,1,0:T(8,128)(2,1)} %get-tuple-element.23), channel_id=1, source_target_pairs={{0,32},{16,48},{32,64},{48,80},{64,96},{80,112},{96,0},{112,16},{1... | collective-permute-start | bytes 1179656 | tf_op jit(solution)/shard_map/ppermute | solution.py:253
  26.8 0.0 collective-permute-start.2
  26.8 0.0 copy-start.2
  26.8 2.2 %collective-permute-start.5 = (bf16[2,384,256]{2,1,0:T(8,128)(2,1)}, bf16[2,384,256]{2,1,0:T(8,128)(2,1)S(1)}, u32[]{:S(2)}, u32[]{:S(2)}) collective-permute-start(bf16[2,384,256]{2,1,0:T(8,128)(2,1)} %get-tuple-element.24), channel_id=1, source_target_pairs={{0,96},{16,112},{32,0},{48,16},{64,32},{80,48},{96,64},{112,80},{1... | collective-permute-start | bytes 1179656 | tf_op jit(solution)/shard_map/ppermute | solution.py:254
  29.0 4.6 %shard_map.57.own_ref = f32[2,384,256]{2,1,0:T(8,128)} custom-call(s32[1]{0:T(128)} %bitcast.me_ref, s32[16]{0:T(128)} %slot_ref.4, f32[64]{0:T(128)} %reshape.37.mpo_ref, bf16[16,4,384,384]{3,2,1,0:T(8,128)(2,1)} %left_hbm.5, bf16[16,384,256]{2,1,0:T(8,128)(2,1)} %site_hbm.5), custom_call_target="tpu_custom_call" | custom-call | flops 1006632960 | bytes 2752512 | tf_op jit(solution)/shard_map/pallas_call | solution.py:98
  33.6 0.0 collective-permute-done.3.far_ref
  33.6 4.7 %collective-permute-done.4.up_ref = bf16[2,384,256]{2,1,0:T(8,128)(2,1)S(1)} collective-permute-done((bf16[2,384,256]{2,1,0:T(8,128)(2,1)}, bf16[2,384,256]{2,1,0:T(8,128)(2,1)S(1)}, u32[]{:S(2)}, u32[]{:S(2)}) %collective-permute-start.4) | collective-permute-done | bytes 393248 | tf_op jit(solution)/shard_map/ppermute | solution.py:253
  38.3 0.0 collective-permute-done.2.other_ref
  38.3 0.2 collective-permute-done.5.down_ref
  38.5 0.0 copy-start
  38.5 1.1 %copy-done = f32[2,384,256]{2,1,0:T(8,128)S(1)} copy-done((f32[2,384,256]{2,1,0:T(8,128)S(1)}, f32[2,384,256]{2,1,0:T(8,128)}, u32[]{:S(2)}) %copy-start) | copy-done | bytes 786456
  39.6 4.2 %shard_map.58 = bf16[8,2,48,256]{3,2,1,0:T(8,128)(2,1)S(1)} custom-call(f32[2,384,256]{2,1,0:T(8,128)S(1)} %copy-done, bf16[2,384,256]{2,1,0:T(8,128)(2,1)S(1)} %collective-permute-done.2.other_ref, bf16[2,384,256]{2,1,0:T(8,128)(2,1)S(1)} %collective-permute-done.3.far_ref, bf16[2,384,256]{2,1,0:T(8,128)(2,1)S(1)} %collective-permute-done.4.up_ref, ...), custom_call_target="tpu_custom_call" | custom-call | flops 3623878656 | bytes 2359296 | tf_op jit(solution)/shard_map/pallas_call | solution.py:206
  43.9 13.6 %all_to_all.10 = bf16[8,2,48,256]{3,2,1,0:T(8,128)(2,1)} all-to-all(bf16[8,2,48,256]{3,2,1,0:T(8,128)(2,1)S(1)} %shard_map.58), channel_id=1, replica_groups=mesh['mpo'=8,'sec'=16] {'mpo'}, dimensions={0} | all-to-all | bytes 786432 | tf_op jit(solution)/shard_map/all_to_all | solution.py:258
  57.4 7.0 %all-to-all-start.1 = ((bf16[16,48,256]{2,1,0:T(8,128)(2,1)}), bf16[16,48,256]{2,1,0:T(8,128)(2,1)S(1)}, u32[]{:S(2)}, u32[]{:S(2)}) async-start(bf16[16,48,256]{2,1,0:T(8,128)(2,1)} %bitcast.1), calls=%async_computation.1 | async-start | bytes 786432 | tf_op jit(solution)/shard_map/all_to_all | solution.py:260
  64.5 0.0 copy-done.2
  64.5 0.1 iota_compare_fusion
  64.6 9.5 %all-to-all-done.1 = bf16[16,48,256]{2,1,0:T(8,128)(2,1)S(1)} async-done(((bf16[16,48,256]{2,1,0:T(8,128)(2,1)}), bf16[16,48,256]{2,1,0:T(8,128)(2,1)S(1)}, u32[]{:S(2)}, u32[]{:S(2)}) %all-to-all-start.1) | async-done | bytes 393248 | tf_op jit(solution)/shard_map/all_to_all | solution.py:260
  74.1 0.8 %broadcast_select_fusion = bf16[16,48,256]{2,1,0:T(8,128)(2,1)} fusion(bf16[16,48,256]{2,1,0:T(8,128)(2,1)S(1)} %all-to-all-done.1, pred[16,256]{1,0:T(8,128)(4,1)S(1)} %iota_compare_fusion), kind=kLoop, calls=%fused_computation.1 | loop fusion | flops 196608 | bytes 790528 | tf_op jit(solution)/shard_map/jit(_where)/select_n | solution.py:262
Async XLA Ops:
  9.7 2.0 %collective-permute-start = (bf16[2,384,256]{2,1,0:T(8,128)(2,1)}, bf16[2,384,256]{2,1,0:T(8,128)(2,1)S(1)}, u32[]{:S(2)}, u32[]{:S(2)}) collective-permute-start(bf16[2,384,256]{2,1,0:T(8,128)(2,1)} %get-tuple-element.16), channel_id=1, source_target_pairs={{0,16},{16,0},{32,48},{48,32},{64,80},{80,64},{96,112},{112,96},{1... | collective-permute-start | bytes 1179656 | tf_op jit(solution)/shard_map/ppermute | solution.py:241
  11.7 5.4 %collective-permute-start.1 = (bf16[4,384,256]{2,1,0:T(8,128)(2,1)}, bf16[4,384,256]{2,1,0:T(8,128)(2,1)S(1)}, u32[]{:S(2)}, u32[]{:S(2)}) collective-permute-start(bf16[4,384,256]{2,1,0:T(8,128)(2,1)} %get-tuple-element.17), channel_id=1, source_target_pairs={{0,16},{16,0},{32,48},{48,32},{64,80},{80,64},{96,112},{112,96},{1... | collective-permute-start | bytes 2359304 | tf_op jit(solution)/shard_map/ppermute | solution.py:243
  13.1 20.5 %collective-permute-start.3 = (bf16[2,384,256]{2,1,0:T(8,128)(2,1)S(1)}, bf16[2,384,256]{2,1,0:T(8,128)(2,1)S(1)}, u32[]{:S(2)}, u32[]{:S(2)}) collective-permute-start(bf16[2,384,256]{2,1,0:T(8,128)(2,1)S(1)} %add_convert_fusion), channel_id=1, source_target_pairs={{0,64},{16,80},{32,96},{48,112},{64,0},{80,16},{96,32},{112,48},{1... | collective-permute-start | bytes 1179656 | tf_op jit(solution)/shard_map/ppermute | solution.py:245
  17.1 0.9 %copy-start.1 = (bf16[4,384,256]{2,1,0:T(8,128)(2,1)}, bf16[4,384,256]{2,1,0:T(8,128)(2,1)S(1)}, u32[]{:S(2)}) copy-start(bf16[4,384,256]{2,1,0:T(8,128)(2,1)S(1)} %collective-permute-done.1.rest_0_.rest_1_) | copy-start | bytes 2359300
  25.7 12.6 %collective-permute-start.4 = (bf16[2,384,256]{2,1,0:T(8,128)(2,1)}, bf16[2,384,256]{2,1,0:T(8,128)(2,1)S(1)}, u32[]{:S(2)}, u32[]{:S(2)}) collective-permute-start(bf16[2,384,256]{2,1,0:T(8,128)(2,1)} %get-tuple-element.23), channel_id=1, source_target_pairs={{0,32},{16,48},{32,64},{48,80},{64,96},{80,112},{96,0},{112,16},{1... | collective-permute-start | bytes 1179656 | tf_op jit(solution)/shard_map/ppermute | solution.py:253
  26.8 11.5 %collective-permute-start.2 = (bf16[2,384,256]{2,1,0:T(8,128)(2,1)}, bf16[2,384,256]{2,1,0:T(8,128)(2,1)S(1)}, u32[]{:S(2)}, u32[]{:S(2)}) collective-permute-start(bf16[2,384,256]{2,1,0:T(8,128)(2,1)} %get-tuple-element.20), channel_id=1, source_target_pairs={{0,16},{16,0},{32,48},{48,32},{64,80},{80,64},{96,112},{112,96},{1... | collective-permute-start | bytes 1179656 | tf_op jit(solution)/shard_map/ppermute | solution.py:255
  26.8 37.7 %copy-start.2 = (s32[16]{0:T(128)S(1)}, s32[16]{0:T(128)}, u32[]{:S(2)}) copy-start(s32[16]{0:T(128)} %param.9) | copy-start | bytes 196
  26.8 11.7 %collective-permute-start.5 = (bf16[2,384,256]{2,1,0:T(8,128)(2,1)}, bf16[2,384,256]{2,1,0:T(8,128)(2,1)S(1)}, u32[]{:S(2)}, u32[]{:S(2)}) collective-permute-start(bf16[2,384,256]{2,1,0:T(8,128)(2,1)} %get-tuple-element.24), channel_id=1, source_target_pairs={{0,96},{16,112},{32,0},{48,16},{64,32},{80,48},{96,64},{112,80},{1... | collective-permute-start | bytes 1179656 | tf_op jit(solution)/shard_map/ppermute | solution.py:254
  38.5 1.1 %copy-start = (f32[2,384,256]{2,1,0:T(8,128)S(1)}, f32[2,384,256]{2,1,0:T(8,128)}, u32[]{:S(2)}) copy-start(f32[2,384,256]{2,1,0:T(8,128)} %shard_map.57.own_ref) | copy-start | bytes 2359300
  57.4 16.7 %all-to-all-start.1 = ((bf16[16,48,256]{2,1,0:T(8,128)(2,1)}), bf16[16,48,256]{2,1,0:T(8,128)(2,1)S(1)}, u32[]{:S(2)}, u32[]{:S(2)}) async-start(bf16[16,48,256]{2,1,0:T(8,128)(2,1)} %bitcast.1), calls=%async_computation.1 | async-start | bytes 786432 | tf_op jit(solution)/shard_map/all_to_all | solution.py:260

commit v3 on v2

--- a/solution.py
+++ b/solution.py
@@ -11,7 +11,7 @@
 EARLY = 4
 PHYS = 4
 CHIPS = 4
-TERM_MIB = 57
+TERM_MIB = 48
 F32, BF16 = jnp.float32, jnp.bfloat16
 
 
@@ -43,12 +43,10 @@
     return jnp.dot(left, stacked_ref[...], preferred_element_type=F32)
 
 
-def term_kernel(me_ref, slot_ref, mpo_ref, left_hbm, site_hbm, *rest, groups):
+def term_kernel(me_ref, slot_ref, mpo_ref, left_hbm, site_ref, *rest, groups):
     added = sum(offset is not None for _, _, offset in groups)
     others, outs = list(rest[:added]), rest[added : added + len(groups)]
-    left_ref, site_ref, mix_ref, stacked_ref, inverse_ref, left_sem, site_sem = rest[
-        added + len(groups) :
-    ]
+    left_ref, mix_ref, stacked_ref, inverse_ref, left_sem = rest[added + len(groups) :]
     wslices = left_ref.shape[1]
     columns = site_ref.shape[2]
     chip, core = lax.div(me_ref[0], 2), lax.rem(me_ref[0], 2)
@@ -59,25 +57,20 @@
         other = None if offset is None else others.pop(0)
         for j, (step, flip) in enumerate(targets):
             member = 2 * lax.rem(chip + step, CHIPS) + (1 - core if flip else core)
-            copies = []
+            parts = []
             for b in range(2):
                 n = 2 * len(work) + b
                 sector = inverse_ref[2 * member + b]
-                copies.append(
-                    pltpu.make_async_copy(site_hbm.at[sector], site_ref.at[n], site_sem.at[n])
-                )
-                copies.append(
-                    pltpu.make_async_copy(left_hbm.at[sector], left_ref.at[n], left_sem.at[n])
-                )
-            for copy in copies:
+                copy = pltpu.make_async_copy(left_hbm.at[sector], left_ref.at[n], left_sem.at[n])
                 copy.start()
-            work.append((copies, outs[g], other, offset, 2 * j))
+                parts.append((copy, sector))
+            work.append((parts, outs[g], other, offset, 2 * j))
     mixing_matrix(mpo_ref, mix_ref, wslices, PHYS, columns // PHYS)
-    for i, (copies, out_ref, other_ref, offset, start) in enumerate(work):
-        for copy in copies:
+    for i, (parts, out_ref, other_ref, offset, start) in enumerate(work):
+        for copy, _ in parts:
             copy.wait()
-        for b in range(2):
-            mix(site_ref[2 * i + b], mix_ref, stacked_ref.at[b])
+        for b, (_, sector) in enumerate(parts):
+            mix(site_ref[sector], mix_ref, stacked_ref.at[b])
         for b in range(2):
             term = contract(left_ref.at[2 * i + b], stacked_ref.at[b])
             if other_ref is not None:
@@ -104,15 +97,13 @@
             jax.ShapeDtypeStruct((2 * len(targets), rows, columns), dtype)
             for targets, dtype, _ in groups
         ],
-        in_specs=[smem, smem, smem, hbm, hbm] + [vmem] * len(others),
+        in_specs=[smem, smem, smem, hbm, vmem] + [vmem] * len(others),
         out_specs=[vmem] * len(groups),
         scratch_shapes=[
             pltpu.VMEM((count, wslices, rows, rows), BF16),
-            pltpu.VMEM((count, rows, columns), BF16),
             pltpu.VMEM((columns, wslices * columns), BF16),
             pltpu.VMEM((2, wslices * rows, columns), BF16),
             pltpu.SMEM((sectors,), jnp.int32),
-            pltpu.SemaphoreType.DMA((count,)),
             pltpu.SemaphoreType.DMA((count,)),
         ],
         compiler_params=pltpu.CompilerParams(vmem_limit_bytes=TERM_MIB * 2**20),

time: 75.3 us -> 70.5 us (0.936)
  Pallas kernels: 24.8 us -> 20.5 us
  other arithmetic: 2.07 us -> 0.95 us
  waiting for transfers between devices: 16.4 us -> 17.5 us
    pallas_call x3, Pallas kernels: 20.6 us -> 16.2 us  [terms(): pl.pallas_call(functools.partial(term_kernel, groups=[(targets, dtype, ot...]
    convert_element_type x1, other arithmetic: 1.22 us -> 0.1 us  [shards(): far = (far_own + far_other.astype(F32)).astype(BF16)]
    ppermute x1, waiting for transfers between devices: 4.66 us -> 5.65 us  [shards(): up = lax.ppermute(up, 'mpo', shift(1))]
  transfers between devices with their start and end apart: 7 -> 7, of which waited for: 4 -> 4; matrix products, arithmetic and copies ran while one was open for 2% -> 0% of each run, Pallas kernels for 16% -> 13%
where the time goes in v3:
time: 70.5 us; the launch traced here: 70.2 us
  Pallas kernels  20.5 us (29%)
  waiting for transfers between devices  17.5 us (25%)
  starting transfers between devices  14.6 us (21%)
  blocking collectives  13.2 us (19%)
  local copies, waits for them, and re-layouts  3.32 us (5%)
  other arithmetic  0.95 us (1%)
    pallas_call x3, Pallas kernels, terms(): pl.pallas_call(functools.partial(term_kernel, groups=[(targets, dtype, ot...  16.2 us
    all_to_all x1, blocking collectives, shards(): lax.all_to_all(result, 'mpo', split_axis=0, concat_axis=0, tiled=True)  13.2 us
    all_to_all x1, waiting for transfers between devices, shards(): lax.all_to_all(rows, 'sec', split_axis=0, concat_axis=0, tiled=True)  9.54 us
    all_to_all x1, starting transfers between devices, shards(): lax.all_to_all(rows, 'sec', split_axis=0, concat_axis=0, tiled=True)  7.03 us
    ppermute x1, waiting for transfers between devices, shards(): up = lax.ppermute(up, 'mpo', shift(1))  5.65 us
    pallas_call x1, Pallas kernels, expansions(): pl.pallas_call(root_kernel, out_shape=jax.ShapeDtypeStruct((parts, count,...  4.25 us
    ppermute x1, starting transfers between devices, shards(): far = lax.ppermute(far, 'mpo', shift(2))  4.05 us
    unnamed x6, local copies, waits for them, and re-layouts  2.54 us
  transfers between devices with their start and end apart: 7, of which 4 were waited for; matrix products, arithmetic and copies ran while one was open for 0% of the time, Pallas kernels for 13%

profile of v3, /device:TPU:0, one launch (start us, length us, event | category | flops | bytes accessed | tf_op | source)
XLA Modules:
  0.0 70.2 jit_solution(18006847750685260649)
XLA Ops:
  0.0 0.8 %reshape.37.mpo_ref = f32[64]{0:T(128)S(1)} reshape(bf16[4,4,4]{2,1,0:T(4,128)(2,1)} %param.7) | data formatting | bytes 384 | tf_op jit(solution)/shard_map/reshape | solution.py:220
  0.8 0.0 copy-start
  0.8 1.9 %copy-done = bf16[16,384,256]{2,1,0:T(8,128)(2,1)S(1)} copy-done((bf16[16,384,256]{2,1,0:T(8,128)(2,1)S(1)}, bf16[16,384,256]{2,1,0:T(8,128)(2,1)}, u32[]{:S(2)}) %copy-start) | copy-done | bytes 3145752
  2.7 0.0 copy-start.1
  2.7 0.7 copy-done.1
  3.3 7.0 %shard_map.55 = (bf16[2,384,256]{2,1,0:T(8,128)(2,1)S(1)}, bf16[4,384,256]{2,1,0:T(8,128)(2,1)S(1)}, f32[2,384,256]{2,1,0:T(8,128)S(1)}) custom-call(s32[1]{0:T(128)} %bitcast.me_ref, s32[16]{0:T(128)S(1)} %copy-done.1, f32[64]{0:T(128)S(1)} %reshape.37.mpo_ref, bf16[16,4,384,384]{3,2,1,0:T(8,128)(2,1)} %left_hbm.5, bf16[16,384,256]{2,1,0:T(8,128)(2,1)S(1)} %copy-done), custom_call_target="tpu_custom_call" | custom-call | flops 4026531840 | bytes 11010048 | tf_op jit(solution)/shard_map/pallas_call | solution.py:91
  10.4 0.1 collective-permute-start
  10.5 1.7 %collective-permute-done = bf16[2,384,256]{2,1,0:T(8,128)(2,1)S(1)} collective-permute-done((bf16[2,384,256]{2,1,0:T(8,128)(2,1)S(1)}, bf16[2,384,256]{2,1,0:T(8,128)(2,1)S(1)}, u32[]{:S(2)}, u32[]{:S(2)}) %collective-permute-start) | collective-permute-done | bytes 393248 | tf_op jit(solution)/shard_map/ppermute | solution.py:232
  12.2 0.1 collective-permute-start.1
  12.3 0.1 add_convert_fusion
  12.4 4.1 %collective-permute-start.3 = (bf16[2,384,256]{2,1,0:T(8,128)(2,1)S(1)}, bf16[2,384,256]{2,1,0:T(8,128)(2,1)S(1)}, u32[]{:S(2)}, u32[]{:S(2)}) collective-permute-start(bf16[2,384,256]{2,1,0:T(8,128)(2,1)S(1)} %add_convert_fusion), channel_id=1, source_target_pairs={{0,64},{16,80},{32,96},{48,112},{64,0},{80,16},{96,32},{112,48},{1... | collective-permute-start | bytes 1179656 | tf_op jit(solution)/shard_map/ppermute | solution.py:236
  16.5 0.0 collective-permute-done.1.rest_0_.rest_1_
  16.5 5.8 %shard_map.56 = (bf16[2,384,256]{2,1,0:T(8,128)(2,1)S(1)}, bf16[2,384,256]{2,1,0:T(8,128)(2,1)S(1)}, bf16[2,384,256]{2,1,0:T(8,128)(2,1)S(1)}) custom-call(s32[1]{0:T(128)} %bitcast.me_ref, s32[16]{0:T(128)S(1)} %copy-done.1, f32[64]{0:T(128)S(1)} %reshape.37.mpo_ref, bf16[16,4,384,384]{3,2,1,0:T(8,128)(2,1)} %left_hbm.5, bf16[16,384,256]{2,1,0:T(8,128)(2,1)S(1)} %copy-done, ...), custom_call_target="tpu_custom_call" | custom-call | flops 3019898880 | bytes 8257536 | tf_op jit(solution)/shard_map/pallas_call | solution.py:91
  22.3 1.1 %collective-permute-start.4 = (bf16[2,384,256]{2,1,0:T(8,128)(2,1)S(1)}, bf16[2,384,256]{2,1,0:T(8,128)(2,1)S(1)}, u32[]{:S(2)}, u32[]{:S(2)}) collective-permute-start(bf16[2,384,256]{2,1,0:T(8,128)(2,1)S(1)} %get-tuple-element.23), channel_id=1, source_target_pairs={{0,32},{16,48},{32,64},{48,80},{64,96},{80,112},{96,0},{112,16},{1... | collective-permute-start | bytes 1179656 | tf_op jit(solution)/shard_map/ppermute | solution.py:244
  23.4 0.0 collective-permute-start.2
  23.4 0.0 copy-start.2
  23.4 2.2 %collective-permute-start.5 = (bf16[2,384,256]{2,1,0:T(8,128)(2,1)S(1)}, bf16[2,384,256]{2,1,0:T(8,128)(2,1)S(1)}, u32[]{:S(2)}, u32[]{:S(2)}) collective-permute-start(bf16[2,384,256]{2,1,0:T(8,128)(2,1)S(1)} %get-tuple-element.24), channel_id=1, source_target_pairs={{0,96},{16,112},{32,0},{48,16},{64,32},{80,48},{96,64},{112,80},{1... | collective-permute-start | bytes 1179656 | tf_op jit(solution)/shard_map/ppermute | solution.py:245
  25.6 3.4 %shard_map.57.own_ref = f32[2,384,256]{2,1,0:T(8,128)S(1)} custom-call(s32[1]{0:T(128)} %bitcast.me_ref, s32[16]{0:T(128)S(1)} %copy-done.1, f32[64]{0:T(128)S(1)} %reshape.37.mpo_ref, bf16[16,4,384,384]{3,2,1,0:T(8,128)(2,1)} %left_hbm.5, bf16[16,384,256]{2,1,0:T(8,128)(2,1)S(1)} %copy-done), custom_call_target="tpu_custom_call" | custom-call | flops 1006632960 | bytes 2752512 | tf_op jit(solution)/shard_map/pallas_call | solution.py:91
  29.0 0.0 collective-permute-done.3.far_ref
  29.0 5.7 %collective-permute-done.4.up_ref = bf16[2,384,256]{2,1,0:T(8,128)(2,1)S(1)} collective-permute-done((bf16[2,384,256]{2,1,0:T(8,128)(2,1)S(1)}, bf16[2,384,256]{2,1,0:T(8,128)(2,1)S(1)}, u32[]{:S(2)}, u32[]{:S(2)}) %collective-permute-start.4) | collective-permute-done | bytes 393248 | tf_op jit(solution)/shard_map/ppermute | solution.py:244
  34.7 0.0 collective-permute-done.2.other_ref
  34.7 0.6 collective-permute-done.5.down_ref
  35.3 4.3 %shard_map.58 = bf16[8,2,48,256]{3,2,1,0:T(8,128)(2,1)S(1)} custom-call(f32[2,384,256]{2,1,0:T(8,128)S(1)} %shard_map.57.own_ref, bf16[2,384,256]{2,1,0:T(8,128)(2,1)S(1)} %collective-permute-done.2.other_ref, bf16[2,384,256]{2,1,0:T(8,128)(2,1)S(1)} %collective-permute-done.3.far_ref, bf16[2,384,256]{2,1,0:T(8,128)(2,1)S(1)} %collective-permute-done.4.up_ref, ...), custom_call_target="tpu_custom_call" | custom-call | flops 3623878656 | bytes 2359296 | tf_op jit(solution)/shard_map/pallas_call | solution.py:197
  39.5 13.2 %all_to_all.10 = bf16[8,2,48,256]{3,2,1,0:T(8,128)(2,1)} all-to-all(bf16[8,2,48,256]{3,2,1,0:T(8,128)(2,1)S(1)} %shard_map.58), channel_id=1, replica_groups=mesh['mpo'=8,'sec'=16] {'mpo'}, dimensions={0} | all-to-all | bytes 786432 | tf_op jit(solution)/shard_map/all_to_all | solution.py:249
  52.7 7.0 %all-to-all-start.1 = ((bf16[16,48,256]{2,1,0:T(8,128)(2,1)}), bf16[16,48,256]{2,1,0:T(8,128)(2,1)S(1)}, u32[]{:S(2)}, u32[]{:S(2)}) async-start(bf16[16,48,256]{2,1,0:T(8,128)(2,1)} %bitcast.1), calls=%async_computation.1 | async-start | bytes 786432 | tf_op jit(solution)/shard_map/all_to_all | solution.py:251
  59.8 0.0 copy-done.2
  59.8 0.1 iota_compare_fusion
  59.8 9.5 %all-to-all-done.1 = bf16[16,48,256]{2,1,0:T(8,128)(2,1)S(1)} async-done(((bf16[16,48,256]{2,1,0:T(8,128)(2,1)}), bf16[16,48,256]{2,1,0:T(8,128)(2,1)S(1)}, u32[]{:S(2)}, u32[]{:S(2)}) %all-to-all-start.1) | async-done | bytes 393248 | tf_op jit(solution)/shard_map/all_to_all | solution.py:251
  69.4 0.8 %broadcast_select_fusion = bf16[16,48,256]{2,1,0:T(8,128)(2,1)} fusion(bf16[16,48,256]{2,1,0:T(8,128)(2,1)S(1)} %all-to-all-done.1, pred[16,256]{1,0:T(8,128)(4,1)S(1)} %iota_compare_fusion), kind=kLoop, calls=%fused_computation.1 | loop fusion | flops 196608 | bytes 790528 | tf_op jit(solution)/shard_map/jit(_where)/select_n | solution.py:253
Async XLA Ops:
  0.8 1.9 %copy-start = (bf16[16,384,256]{2,1,0:T(8,128)(2,1)S(1)}, bf16[16,384,256]{2,1,0:T(8,128)(2,1)}, u32[]{:S(2)}) copy-start(bf16[16,384,256]{2,1,0:T(8,128)(2,1)} %site_ref.5) | copy-start | bytes 9437188
  2.7 0.7 copy-start.1
  10.4 1.8 %collective-permute-start = (bf16[2,384,256]{2,1,0:T(8,128)(2,1)S(1)}, bf16[2,384,256]{2,1,0:T(8,128)(2,1)S(1)}, u32[]{:S(2)}, u32[]{:S(2)}) collective-permute-start(bf16[2,384,256]{2,1,0:T(8,128)(2,1)S(1)} %get-tuple-element.16), channel_id=1, source_target_pairs={{0,16},{16,0},{32,48},{48,32},{64,80},{80,64},{96,112},{112,96},{1... | collective-permute-start | bytes 1179656 | tf_op jit(solution)/shard_map/ppermute | solution.py:232
  12.2 4.3 %collective-permute-start.1 = (bf16[4,384,256]{2,1,0:T(8,128)(2,1)S(1)}, bf16[4,384,256]{2,1,0:T(8,128)(2,1)S(1)}, u32[]{:S(2)}, u32[]{:S(2)}) collective-permute-start(bf16[4,384,256]{2,1,0:T(8,128)(2,1)S(1)} %get-tuple-element.17), channel_id=1, source_target_pairs={{0,16},{16,0},{32,48},{48,32},{64,80},{80,64},{96,112},{112,96},{1... | collective-permute-start | bytes 2359304 | tf_op jit(solution)/shard_map/ppermute | solution.py:234
  12.4 16.6 %collective-permute-start.3 = (bf16[2,384,256]{2,1,0:T(8,128)(2,1)S(1)}, bf16[2,384,256]{2,1,0:T(8,128)(2,1)S(1)}, u32[]{:S(2)}, u32[]{:S(2)}) collective-permute-start(bf16[2,384,256]{2,1,0:T(8,128)(2,1)S(1)} %add_convert_fusion), channel_id=1, source_target_pairs={{0,64},{16,80},{32,96},{48,112},{64,0},{80,16},{96,32},{112,48},{1... | collective-permute-start | bytes 1179656 | tf_op jit(solution)/shard_map/ppermute | solution.py:236
  22.3 12.4 %collective-permute-start.4 = (bf16[2,384,256]{2,1,0:T(8,128)(2,1)S(1)}, bf16[2,384,256]{2,1,0:T(8,128)(2,1)S(1)}, u32[]{:S(2)}, u32[]{:S(2)}) collective-permute-start(bf16[2,384,256]{2,1,0:T(8,128)(2,1)S(1)} %get-tuple-element.23), channel_id=1, source_target_pairs={{0,32},{16,48},{32,64},{48,80},{64,96},{80,112},{96,0},{112,16},{1... | collective-permute-start | bytes 1179656 | tf_op jit(solution)/shard_map/ppermute | solution.py:244
  23.4 11.3 %collective-permute-start.2 = (bf16[2,384,256]{2,1,0:T(8,128)(2,1)S(1)}, bf16[2,384,256]{2,1,0:T(8,128)(2,1)S(1)}, u32[]{:S(2)}, u32[]{:S(2)}) collective-permute-start(bf16[2,384,256]{2,1,0:T(8,128)(2,1)S(1)} %get-tuple-element.20), channel_id=1, source_target_pairs={{0,16},{16,0},{32,48},{48,32},{64,80},{80,64},{96,112},{112,96},{1... | collective-permute-start | bytes 1179656 | tf_op jit(solution)/shard_map/ppermute | solution.py:246
  23.4 36.4 %copy-start.2 = (s32[16]{0:T(128)S(1)}, s32[16]{0:T(128)}, u32[]{:S(2)}) copy-start(s32[16]{0:T(128)} %param.9) | copy-start | bytes 196
  23.4 11.9 %collective-permute-start.5 = (bf16[2,384,256]{2,1,0:T(8,128)(2,1)S(1)}, bf16[2,384,256]{2,1,0:T(8,128)(2,1)S(1)}, u32[]{:S(2)}, u32[]{:S(2)}) collective-permute-start(bf16[2,384,256]{2,1,0:T(8,128)(2,1)S(1)} %get-tuple-element.24), channel_id=1, source_target_pairs={{0,96},{16,112},{32,0},{48,16},{64,32},{80,48},{96,64},{112,80},{1... | collective-permute-start | bytes 1179656 | tf_op jit(solution)/shard_map/ppermute | solution.py:245
  52.7 16.7 %all-to-all-start.1 = ((bf16[16,48,256]{2,1,0:T(8,128)(2,1)}), bf16[16,48,256]{2,1,0:T(8,128)(2,1)S(1)}, u32[]{:S(2)}, u32[]{:S(2)}) async-start(bf16[16,48,256]{2,1,0:T(8,128)(2,1)} %bitcast.1), calls=%async_computation.1 | async-start | bytes 786432 | tf_op jit(solution)/shard_map/all_to_all | solution.py:251

commit v4 on v3

--- a/solution.py
+++ b/solution.py
@@ -178,13 +178,24 @@
                     for b in sectors
                 ]
         else:
-            halves = [split(current[b]) for b in sectors]
-            others = [split(partner[b]) for b in sectors]
-            factor = [1.5 * identity - 0.5 * product(others[b], halves[b]) for b in sectors]
-            pairs = [split(factor[b]) for b in sectors]
+            rounded = [current[b].astype(BF16) for b in sectors]
+            others = [partner[b].astype(BF16) for b in sectors]
+            away = [
+                (
+                    0.5 * identity
+                    - 0.5 * jnp.dot(others[b], rounded[b], preferred_element_type=F32)
+                ).astype(BF16)
+                for b in sectors
+            ]
             if repeat < ITERS - 1:
-                current = [product(halves[b], pairs[b]) for b in sectors]
-            partner = [product(pairs[b], others[b]) for b in sectors]
+                current = [
+                    current[b] + jnp.dot(rounded[b], away[b], preferred_element_type=F32)
+                    for b in sectors
+                ]
+            partner = [
+                partner[b] + jnp.dot(away[b], others[b], preferred_element_type=F32)
+                for b in sectors
+            ]
     for b in sectors:
         result = (product(term[b], split(partner[b] * scale[b]))).astype(BF16)
         for m in range(parts):

time: 70.5 us -> 69.8 us (0.990)
  Pallas kernels: 20.5 us -> 19.7 us
    pallas_call x1, Pallas kernels: 4.25 us -> 3.49 us  [expansions(): pl.pallas_call(root_kernel, out_shape=jax.ShapeDtypeStruct((parts, count,...]
where the time goes in v4:
time: 69.8 us; the launch traced here: 69.4 us
  Pallas kernels  19.7 us (28%)
  waiting for transfers between devices  17.5 us (25%)
  starting transfers between devices  14.6 us (21%)
  blocking collectives  13.2 us (19%)
  local copies, waits for them, and re-layouts  3.32 us (5%)
  other arithmetic  0.95 us (1%)
    pallas_call x3, Pallas kernels, terms(): pl.pallas_call(functools.partial(term_kernel, groups=[(targets, dtype, ot...  16.2 us
    all_to_all x1, blocking collectives, shards(): lax.all_to_all(result, 'mpo', split_axis=0, concat_axis=0, tiled=True)  13.2 us
    all_to_all x1, waiting for transfers between devices, shards(): lax.all_to_all(rows, 'sec', split_axis=0, concat_axis=0, tiled=True)  9.54 us
    all_to_all x1, starting transfers between devices, shards(): lax.all_to_all(rows, 'sec', split_axis=0, concat_axis=0, tiled=True)  7.03 us
    ppermute x1, waiting for transfers between devices, shards(): up = lax.ppermute(up, 'mpo', shift(1))  5.65 us
    ppermute x1, starting transfers between devices, shards(): far = lax.ppermute(far, 'mpo', shift(2))  4.05 us
    pallas_call x1, Pallas kernels, expansions(): pl.pallas_call(root_kernel, out_shape=jax.ShapeDtypeStruct((parts, count,...  3.49 us
    unnamed x6, local copies, waits for them, and re-layouts  2.54 us
  transfers between devices with their start and end apart: 7, of which 4 were waited for; matrix products, arithmetic and copies ran while one was open for 0% of the time, Pallas kernels for 13%

profile of v4, /device:TPU:0, one launch (start us, length us, event | category | flops | bytes accessed | tf_op | source)
XLA Modules:
  0.0 69.4 jit_solution(8418993002762022306)
XLA Ops:
  0.0 0.8 %reshape.37.mpo_ref = f32[64]{0:T(128)S(1)} reshape(bf16[4,4,4]{2,1,0:T(4,128)(2,1)} %param.7) | data formatting | bytes 384 | tf_op jit(solution)/shard_map/reshape | solution.py:231
  0.8 0.0 copy-start
  0.8 1.9 %copy-done = bf16[16,384,256]{2,1,0:T(8,128)(2,1)S(1)} copy-done((bf16[16,384,256]{2,1,0:T(8,128)(2,1)S(1)}, bf16[16,384,256]{2,1,0:T(8,128)(2,1)}, u32[]{:S(2)}) %copy-start) | copy-done | bytes 3145752
  2.7 0.0 copy-start.1
  2.7 0.7 copy-done.1
  3.3 7.0 %shard_map.55 = (bf16[2,384,256]{2,1,0:T(8,128)(2,1)S(1)}, bf16[4,384,256]{2,1,0:T(8,128)(2,1)S(1)}, f32[2,384,256]{2,1,0:T(8,128)S(1)}) custom-call(s32[1]{0:T(128)} %bitcast.me_ref, s32[16]{0:T(128)S(1)} %copy-done.1, f32[64]{0:T(128)S(1)} %reshape.37.mpo_ref, bf16[16,4,384,384]{3,2,1,0:T(8,128)(2,1)} %left_hbm.5, bf16[16,384,256]{2,1,0:T(8,128)(2,1)S(1)} %copy-done), custom_call_target="tpu_custom_call" | custom-call | flops 4026531840 | bytes 11010048 | tf_op jit(solution)/shard_map/pallas_call | solution.py:91
  10.4 0.1 collective-permute-start
  10.5 1.7 %collective-permute-done = bf16[2,384,256]{2,1,0:T(8,128)(2,1)S(1)} collective-permute-done((bf16[2,384,256]{2,1,0:T(8,128)(2,1)S(1)}, bf16[2,384,256]{2,1,0:T(8,128)(2,1)S(1)}, u32[]{:S(2)}, u32[]{:S(2)}) %collective-permute-start) | collective-permute-done | bytes 393248 | tf_op jit(solution)/shard_map/ppermute | solution.py:243
  12.2 0.1 collective-permute-start.1
  12.3 0.1 add_convert_fusion
  12.4 4.1 %collective-permute-start.3 = (bf16[2,384,256]{2,1,0:T(8,128)(2,1)S(1)}, bf16[2,384,256]{2,1,0:T(8,128)(2,1)S(1)}, u32[]{:S(2)}, u32[]{:S(2)}) collective-permute-start(bf16[2,384,256]{2,1,0:T(8,128)(2,1)S(1)} %add_convert_fusion), channel_id=1, source_target_pairs={{0,64},{16,80},{32,96},{48,112},{64,0},{80,16},{96,32},{112,48},{1... | collective-permute-start | bytes 1179656 | tf_op jit(solution)/shard_map/ppermute | solution.py:247
  16.5 0.0 collective-permute-done.1.rest_0_.rest_1_
  16.5 5.8 %shard_map.56 = (bf16[2,384,256]{2,1,0:T(8,128)(2,1)S(1)}, bf16[2,384,256]{2,1,0:T(8,128)(2,1)S(1)}, bf16[2,384,256]{2,1,0:T(8,128)(2,1)S(1)}) custom-call(s32[1]{0:T(128)} %bitcast.me_ref, s32[16]{0:T(128)S(1)} %copy-done.1, f32[64]{0:T(128)S(1)} %reshape.37.mpo_ref, bf16[16,4,384,384]{3,2,1,0:T(8,128)(2,1)} %left_hbm.5, bf16[16,384,256]{2,1,0:T(8,128)(2,1)S(1)} %copy-done, ...), custom_call_target="tpu_custom_call" | custom-call | flops 3019898880 | bytes 8257536 | tf_op jit(solution)/shard_map/pallas_call | solution.py:91
  22.3 1.1 %collective-permute-start.4 = (bf16[2,384,256]{2,1,0:T(8,128)(2,1)S(1)}, bf16[2,384,256]{2,1,0:T(8,128)(2,1)S(1)}, u32[]{:S(2)}, u32[]{:S(2)}) collective-permute-start(bf16[2,384,256]{2,1,0:T(8,128)(2,1)S(1)} %get-tuple-element.23), channel_id=1, source_target_pairs={{0,32},{16,48},{32,64},{48,80},{64,96},{80,112},{96,0},{112,16},{1... | collective-permute-start | bytes 1179656 | tf_op jit(solution)/shard_map/ppermute | solution.py:255
  23.4 0.0 collective-permute-start.2
  23.4 0.0 copy-start.2
  23.4 2.2 %collective-permute-start.5 = (bf16[2,384,256]{2,1,0:T(8,128)(2,1)S(1)}, bf16[2,384,256]{2,1,0:T(8,128)(2,1)S(1)}, u32[]{:S(2)}, u32[]{:S(2)}) collective-permute-start(bf16[2,384,256]{2,1,0:T(8,128)(2,1)S(1)} %get-tuple-element.24), channel_id=1, source_target_pairs={{0,96},{16,112},{32,0},{48,16},{64,32},{80,48},{96,64},{112,80},{1... | collective-permute-start | bytes 1179656 | tf_op jit(solution)/shard_map/ppermute | solution.py:256
  25.6 3.4 %shard_map.57.own_ref = f32[2,384,256]{2,1,0:T(8,128)S(1)} custom-call(s32[1]{0:T(128)} %bitcast.me_ref, s32[16]{0:T(128)S(1)} %copy-done.1, f32[64]{0:T(128)S(1)} %reshape.37.mpo_ref, bf16[16,4,384,384]{3,2,1,0:T(8,128)(2,1)} %left_hbm.5, bf16[16,384,256]{2,1,0:T(8,128)(2,1)S(1)} %copy-done), custom_call_target="tpu_custom_call" | custom-call | flops 1006632960 | bytes 2752512 | tf_op jit(solution)/shard_map/pallas_call | solution.py:91
  29.0 0.0 collective-permute-done.3.far_ref
  29.0 5.7 %collective-permute-done.4.up_ref = bf16[2,384,256]{2,1,0:T(8,128)(2,1)S(1)} collective-permute-done((bf16[2,384,256]{2,1,0:T(8,128)(2,1)S(1)}, bf16[2,384,256]{2,1,0:T(8,128)(2,1)S(1)}, u32[]{:S(2)}, u32[]{:S(2)}) %collective-permute-start.4) | collective-permute-done | bytes 393248 | tf_op jit(solution)/shard_map/ppermute | solution.py:255
  34.7 0.0 collective-permute-done.2.other_ref
  34.7 0.6 collective-permute-done.5.down_ref
  35.3 3.5 %shard_map.58 = bf16[8,2,48,256]{3,2,1,0:T(8,128)(2,1)S(1)} custom-call(f32[2,384,256]{2,1,0:T(8,128)S(1)} %shard_map.57.own_ref, bf16[2,384,256]{2,1,0:T(8,128)(2,1)S(1)} %collective-permute-done.2.other_ref, bf16[2,384,256]{2,1,0:T(8,128)(2,1)S(1)} %collective-permute-done.3.far_ref, bf16[2,384,256]{2,1,0:T(8,128)(2,1)S(1)} %collective-permute-done.4.up_ref, ...), custom_call_target="tpu_custom_call" | custom-call | flops 3623878656 | bytes 2359296 | tf_op jit(solution)/shard_map/pallas_call | solution.py:208
  38.8 13.2 %all_to_all.10 = bf16[8,2,48,256]{3,2,1,0:T(8,128)(2,1)} all-to-all(bf16[8,2,48,256]{3,2,1,0:T(8,128)(2,1)S(1)} %shard_map.58), channel_id=1, replica_groups=mesh['mpo'=8,'sec'=16] {'mpo'}, dimensions={0} | all-to-all | bytes 786432 | tf_op jit(solution)/shard_map/all_to_all | solution.py:260
  52.0 7.0 %all-to-all-start.1 = ((bf16[16,48,256]{2,1,0:T(8,128)(2,1)}), bf16[16,48,256]{2,1,0:T(8,128)(2,1)S(1)}, u32[]{:S(2)}, u32[]{:S(2)}) async-start(bf16[16,48,256]{2,1,0:T(8,128)(2,1)} %bitcast.1), calls=%async_computation.1 | async-start | bytes 786432 | tf_op jit(solution)/shard_map/all_to_all | solution.py:262
  59.0 0.0 copy-done.2
  59.0 0.1 iota_compare_fusion
  59.1 9.5 %all-to-all-done.1 = bf16[16,48,256]{2,1,0:T(8,128)(2,1)S(1)} async-done(((bf16[16,48,256]{2,1,0:T(8,128)(2,1)}), bf16[16,48,256]{2,1,0:T(8,128)(2,1)S(1)}, u32[]{:S(2)}, u32[]{:S(2)}) %all-to-all-start.1) | async-done | bytes 393248 | tf_op jit(solution)/shard_map/all_to_all | solution.py:262
  68.6 0.8 %broadcast_select_fusion = bf16[16,48,256]{2,1,0:T(8,128)(2,1)} fusion(bf16[16,48,256]{2,1,0:T(8,128)(2,1)S(1)} %all-to-all-done.1, pred[16,256]{1,0:T(8,128)(4,1)S(1)} %iota_compare_fusion), kind=kLoop, calls=%fused_computation.1 | loop fusion | flops 196608 | bytes 790528 | tf_op jit(solution)/shard_map/jit(_where)/select_n | solution.py:264
Async XLA Ops:
  0.8 1.9 %copy-start = (bf16[16,384,256]{2,1,0:T(8,128)(2,1)S(1)}, bf16[16,384,256]{2,1,0:T(8,128)(2,1)}, u32[]{:S(2)}) copy-start(bf16[16,384,256]{2,1,0:T(8,128)(2,1)} %site_ref.5) | copy-start | bytes 9437188
  2.7 0.7 copy-start.1
  10.4 1.8 %collective-permute-start = (bf16[2,384,256]{2,1,0:T(8,128)(2,1)S(1)}, bf16[2,384,256]{2,1,0:T(8,128)(2,1)S(1)}, u32[]{:S(2)}, u32[]{:S(2)}) collective-permute-start(bf16[2,384,256]{2,1,0:T(8,128)(2,1)S(1)} %get-tuple-element.16), channel_id=1, source_target_pairs={{0,16},{16,0},{32,48},{48,32},{64,80},{80,64},{96,112},{112,96},{1... | collective-permute-start | bytes 1179656 | tf_op jit(solution)/shard_map/ppermute | solution.py:243
  12.2 4.3 %collective-permute-start.1 = (bf16[4,384,256]{2,1,0:T(8,128)(2,1)S(1)}, bf16[4,384,256]{2,1,0:T(8,128)(2,1)S(1)}, u32[]{:S(2)}, u32[]{:S(2)}) collective-permute-start(bf16[4,384,256]{2,1,0:T(8,128)(2,1)S(1)} %get-tuple-element.17), channel_id=1, source_target_pairs={{0,16},{16,0},{32,48},{48,32},{64,80},{80,64},{96,112},{112,96},{1... | collective-permute-start | bytes 2359304 | tf_op jit(solution)/shard_map/ppermute | solution.py:245
  12.4 16.6 %collective-permute-start.3 = (bf16[2,384,256]{2,1,0:T(8,128)(2,1)S(1)}, bf16[2,384,256]{2,1,0:T(8,128)(2,1)S(1)}, u32[]{:S(2)}, u32[]{:S(2)}) collective-permute-start(bf16[2,384,256]{2,1,0:T(8,128)(2,1)S(1)} %add_convert_fusion), channel_id=1, source_target_pairs={{0,64},{16,80},{32,96},{48,112},{64,0},{80,16},{96,32},{112,48},{1... | collective-permute-start | bytes 1179656 | tf_op jit(solution)/shard_map/ppermute | solution.py:247
  22.3 12.4 %collective-permute-start.4 = (bf16[2,384,256]{2,1,0:T(8,128)(2,1)S(1)}, bf16[2,384,256]{2,1,0:T(8,128)(2,1)S(1)}, u32[]{:S(2)}, u32[]{:S(2)}) collective-permute-start(bf16[2,384,256]{2,1,0:T(8,128)(2,1)S(1)} %get-tuple-element.23), channel_id=1, source_target_pairs={{0,32},{16,48},{32,64},{48,80},{64,96},{80,112},{96,0},{112,16},{1... | collective-permute-start | bytes 1179656 | tf_op jit(solution)/shard_map/ppermute | solution.py:255
  23.4 11.3 %collective-permute-start.2 = (bf16[2,384,256]{2,1,0:T(8,128)(2,1)S(1)}, bf16[2,384,256]{2,1,0:T(8,128)(2,1)S(1)}, u32[]{:S(2)}, u32[]{:S(2)}) collective-permute-start(bf16[2,384,256]{2,1,0:T(8,128)(2,1)S(1)} %get-tuple-element.20), channel_id=1, source_target_pairs={{0,16},{16,0},{32,48},{48,32},{64,80},{80,64},{96,112},{112,96},{1... | collective-permute-start | bytes 1179656 | tf_op jit(solution)/shard_map/ppermute | solution.py:257
  23.4 35.6 %copy-start.2 = (s32[16]{0:T(128)S(1)}, s32[16]{0:T(128)}, u32[]{:S(2)}) copy-start(s32[16]{0:T(128)} %param.9) | copy-start | bytes 196
  23.4 11.9 %collective-permute-start.5 = (bf16[2,384,256]{2,1,0:T(8,128)(2,1)S(1)}, bf16[2,384,256]{2,1,0:T(8,128)(2,1)S(1)}, u32[]{:S(2)}, u32[]{:S(2)}) collective-permute-start(bf16[2,384,256]{2,1,0:T(8,128)(2,1)S(1)} %get-tuple-element.24), channel_id=1, source_target_pairs={{0,96},{16,112},{32,0},{48,16},{64,32},{80,48},{96,64},{112,80},{1... | collective-permute-start | bytes 1179656 | tf_op jit(solution)/shard_map/ppermute | solution.py:256
  52.0 16.7 %all-to-all-start.1 = ((bf16[16,48,256]{2,1,0:T(8,128)(2,1)}), bf16[16,48,256]{2,1,0:T(8,128)(2,1)S(1)}, u32[]{:S(2)}, u32[]{:S(2)}) async-start(bf16[16,48,256]{2,1,0:T(8,128)(2,1)} %bitcast.1), calls=%async_computation.1 | async-start | bytes 786432 | tf_op jit(solution)/shard_map/all_to_all | solution.py:262

commit v5 on v4

--- a/solution.py
+++ b/solution.py
@@ -142,12 +142,14 @@
             + down_ref[b].astype(F32)
         )
         high, low = split(total)
-        gram = lax.dot_general(
-            jnp.concatenate([high, high, low], axis=0),
-            jnp.concatenate([high, low, high], axis=0),
+        both = lax.dot_general(
+            high,
+            jnp.concatenate([high, low], axis=1),
             (((0,), (0,)), ((), ())),
             preferred_element_type=F32,
         )
+        cross = both[:, columns:]
+        gram = both[:, :columns] + (cross + cross.T)
         norm = jnp.sqrt(jnp.sum(gram * gram, keepdims=True))
         term.append((high, low))
         current.append(gram / norm)

time: 69.8 us -> 69.6 us (level)
  no operation moved by 1% of the time
where the time goes in v5:
time: 69.6 us; the launch traced here: 69.2 us
  Pallas kernels  19.5 us (28%)
  waiting for transfers between devices  17.5 us (25%)
  starting transfers between devices  14.6 us (21%)
  blocking collectives  13.2 us (19%)
  local copies, waits for them, and re-layouts  3.32 us (5%)
  other arithmetic  0.95 us (1%)
    pallas_call x3, Pallas kernels, terms(): pl.pallas_call(functools.partial(term_kernel, groups=[(targets, dtype, ot...  16.2 us
    all_to_all x1, blocking collectives, shards(): lax.all_to_all(result, 'mpo', split_axis=0, concat_axis=0, tiled=True)  13.2 us
    all_to_all x1, waiting for transfers between devices, shards(): lax.all_to_all(rows, 'sec', split_axis=0, concat_axis=0, tiled=True)  9.54 us
    all_to_all x1, starting transfers between devices, shards(): lax.all_to_all(rows, 'sec', split_axis=0, concat_axis=0, tiled=True)  7.03 us
    ppermute x1, waiting for transfers between devices, shards(): up = lax.ppermute(up, 'mpo', shift(1))  5.65 us
    ppermute x1, starting transfers between devices, shards(): far = lax.ppermute(far, 'mpo', shift(2))  4.05 us
    pallas_call x1, Pallas kernels, expansions(): pl.pallas_call(root_kernel, out_shape=jax.ShapeDtypeStruct((parts, count,...  3.3 us
    unnamed x6, local copies, waits for them, and re-layouts  2.54 us
  transfers between devices with their start and end apart: 7, of which 4 were waited for; matrix products, arithmetic and copies ran while one was open for 0% of the time, Pallas kernels for 13%

profile of v5, /device:TPU:0, one launch (start us, length us, event | category | flops | bytes accessed | tf_op | source)
XLA Modules:
  0.0 69.2 jit_solution(3992422126549496126)
XLA Ops:
  0.0 0.8 %reshape.37.mpo_ref = f32[64]{0:T(128)S(1)} reshape(bf16[4,4,4]{2,1,0:T(4,128)(2,1)} %param.7) | data formatting | bytes 384 | tf_op jit(solution)/shard_map/reshape | solution.py:233
  0.8 0.0 copy-start
  0.8 1.9 %copy-done = bf16[16,384,256]{2,1,0:T(8,128)(2,1)S(1)} copy-done((bf16[16,384,256]{2,1,0:T(8,128)(2,1)S(1)}, bf16[16,384,256]{2,1,0:T(8,128)(2,1)}, u32[]{:S(2)}) %copy-start) | copy-done | bytes 3145752
  2.7 0.0 copy-start.1
  2.7 0.7 copy-done.1
  3.3 7.0 %shard_map.55 = (bf16[2,384,256]{2,1,0:T(8,128)(2,1)S(1)}, bf16[4,384,256]{2,1,0:T(8,128)(2,1)S(1)}, f32[2,384,256]{2,1,0:T(8,128)S(1)}) custom-call(s32[1]{0:T(128)} %bitcast.me_ref, s32[16]{0:T(128)S(1)} %copy-done.1, f32[64]{0:T(128)S(1)} %reshape.37.mpo_ref, bf16[16,4,384,384]{3,2,1,0:T(8,128)(2,1)} %left_hbm.5, bf16[16,384,256]{2,1,0:T(8,128)(2,1)S(1)} %copy-done), custom_call_target="tpu_custom_call" | custom-call | flops 4026531840 | bytes 11010048 | tf_op jit(solution)/shard_map/pallas_call | solution.py:91
  10.4 0.1 collective-permute-start
  10.5 1.7 %collective-permute-done = bf16[2,384,256]{2,1,0:T(8,128)(2,1)S(1)} collective-permute-done((bf16[2,384,256]{2,1,0:T(8,128)(2,1)S(1)}, bf16[2,384,256]{2,1,0:T(8,128)(2,1)S(1)}, u32[]{:S(2)}, u32[]{:S(2)}) %collective-permute-start) | collective-permute-done | bytes 393248 | tf_op jit(solution)/shard_map/ppermute | solution.py:245
  12.2 0.1 collective-permute-start.1
  12.3 0.1 add_convert_fusion
  12.4 4.1 %collective-permute-start.3 = (bf16[2,384,256]{2,1,0:T(8,128)(2,1)S(1)}, bf16[2,384,256]{2,1,0:T(8,128)(2,1)S(1)}, u32[]{:S(2)}, u32[]{:S(2)}) collective-permute-start(bf16[2,384,256]{2,1,0:T(8,128)(2,1)S(1)} %add_convert_fusion), channel_id=1, source_target_pairs={{0,64},{16,80},{32,96},{48,112},{64,0},{80,16},{96,32},{112,48},{1... | collective-permute-start | bytes 1179656 | tf_op jit(solution)/shard_map/ppermute | solution.py:249
  16.5 0.0 collective-permute-done.1.rest_0_.rest_1_
  16.5 5.8 %shard_map.56 = (bf16[2,384,256]{2,1,0:T(8,128)(2,1)S(1)}, bf16[2,384,256]{2,1,0:T(8,128)(2,1)S(1)}, bf16[2,384,256]{2,1,0:T(8,128)(2,1)S(1)}) custom-call(s32[1]{0:T(128)} %bitcast.me_ref, s32[16]{0:T(128)S(1)} %copy-done.1, f32[64]{0:T(128)S(1)} %reshape.37.mpo_ref, bf16[16,4,384,384]{3,2,1,0:T(8,128)(2,1)} %left_hbm.5, bf16[16,384,256]{2,1,0:T(8,128)(2,1)S(1)} %copy-done, ...), custom_call_target="tpu_custom_call" | custom-call | flops 3019898880 | bytes 8257536 | tf_op jit(solution)/shard_map/pallas_call | solution.py:91
  22.3 1.1 %collective-permute-start.4 = (bf16[2,384,256]{2,1,0:T(8,128)(2,1)S(1)}, bf16[2,384,256]{2,1,0:T(8,128)(2,1)S(1)}, u32[]{:S(2)}, u32[]{:S(2)}) collective-permute-start(bf16[2,384,256]{2,1,0:T(8,128)(2,1)S(1)} %get-tuple-element.23), channel_id=1, source_target_pairs={{0,32},{16,48},{32,64},{48,80},{64,96},{80,112},{96,0},{112,16},{1... | collective-permute-start | bytes 1179656 | tf_op jit(solution)/shard_map/ppermute | solution.py:257
  23.4 0.0 collective-permute-start.2
  23.4 0.0 copy-start.2
  23.4 2.2 %collective-permute-start.5 = (bf16[2,384,256]{2,1,0:T(8,128)(2,1)S(1)}, bf16[2,384,256]{2,1,0:T(8,128)(2,1)S(1)}, u32[]{:S(2)}, u32[]{:S(2)}) collective-permute-start(bf16[2,384,256]{2,1,0:T(8,128)(2,1)S(1)} %get-tuple-element.24), channel_id=1, source_target_pairs={{0,96},{16,112},{32,0},{48,16},{64,32},{80,48},{96,64},{112,80},{1... | collective-permute-start | bytes 1179656 | tf_op jit(solution)/shard_map/ppermute | solution.py:258
  25.6 3.4 %shard_map.57.own_ref = f32[2,384,256]{2,1,0:T(8,128)S(1)} custom-call(s32[1]{0:T(128)} %bitcast.me_ref, s32[16]{0:T(128)S(1)} %copy-done.1, f32[64]{0:T(128)S(1)} %reshape.37.mpo_ref, bf16[16,4,384,384]{3,2,1,0:T(8,128)(2,1)} %left_hbm.5, bf16[16,384,256]{2,1,0:T(8,128)(2,1)S(1)} %copy-done), custom_call_target="tpu_custom_call" | custom-call | flops 1006632960 | bytes 2752512 | tf_op jit(solution)/shard_map/pallas_call | solution.py:91
  29.0 0.0 collective-permute-done.3.far_ref
  29.0 5.7 %collective-permute-done.4.up_ref = bf16[2,384,256]{2,1,0:T(8,128)(2,1)S(1)} collective-permute-done((bf16[2,384,256]{2,1,0:T(8,128)(2,1)S(1)}, bf16[2,384,256]{2,1,0:T(8,128)(2,1)S(1)}, u32[]{:S(2)}, u32[]{:S(2)}) %collective-permute-start.4) | collective-permute-done | bytes 393248 | tf_op jit(solution)/shard_map/ppermute | solution.py:257
  34.7 0.0 collective-permute-done.2.other_ref
  34.7 0.6 collective-permute-done.5.down_ref
  35.3 3.3 %shard_map.58 = bf16[8,2,48,256]{3,2,1,0:T(8,128)(2,1)S(1)} custom-call(f32[2,384,256]{2,1,0:T(8,128)S(1)} %shard_map.57.own_ref, bf16[2,384,256]{2,1,0:T(8,128)(2,1)S(1)} %collective-permute-done.2.other_ref, bf16[2,384,256]{2,1,0:T(8,128)(2,1)S(1)} %collective-permute-done.3.far_ref, bf16[2,384,256]{2,1,0:T(8,128)(2,1)S(1)} %collective-permute-done.4.up_ref, ...), custom_call_target="tpu_custom_call" | custom-call | flops 3623878656 | bytes 2359296 | tf_op jit(solution)/shard_map/pallas_call | solution.py:210
  38.6 13.2 %all_to_all.10 = bf16[8,2,48,256]{3,2,1,0:T(8,128)(2,1)} all-to-all(bf16[8,2,48,256]{3,2,1,0:T(8,128)(2,1)S(1)} %shard_map.58), channel_id=1, replica_groups=mesh['mpo'=8,'sec'=16] {'mpo'}, dimensions={0} | all-to-all | bytes 786432 | tf_op jit(solution)/shard_map/all_to_all | solution.py:262
  51.8 7.0 %all-to-all-start.1 = ((bf16[16,48,256]{2,1,0:T(8,128)(2,1)}), bf16[16,48,256]{2,1,0:T(8,128)(2,1)S(1)}, u32[]{:S(2)}, u32[]{:S(2)}) async-start(bf16[16,48,256]{2,1,0:T(8,128)(2,1)} %bitcast.1), calls=%async_computation.1 | async-start | bytes 786432 | tf_op jit(solution)/shard_map/all_to_all | solution.py:264
  58.8 0.0 copy-done.2
  58.8 0.1 iota_compare_fusion
  58.9 9.5 %all-to-all-done.1 = bf16[16,48,256]{2,1,0:T(8,128)(2,1)S(1)} async-done(((bf16[16,48,256]{2,1,0:T(8,128)(2,1)}), bf16[16,48,256]{2,1,0:T(8,128)(2,1)S(1)}, u32[]{:S(2)}, u32[]{:S(2)}) %all-to-all-start.1) | async-done | bytes 393248 | tf_op jit(solution)/shard_map/all_to_all | solution.py:264
  68.4 0.8 %broadcast_select_fusion = bf16[16,48,256]{2,1,0:T(8,128)(2,1)} fusion(bf16[16,48,256]{2,1,0:T(8,128)(2,1)S(1)} %all-to-all-done.1, pred[16,256]{1,0:T(8,128)(4,1)S(1)} %iota_compare_fusion), kind=kLoop, calls=%fused_computation.1 | loop fusion | flops 196608 | bytes 790528 | tf_op jit(solution)/shard_map/jit(_where)/select_n | solution.py:266
Async XLA Ops:
  0.8 1.9 %copy-start = (bf16[16,384,256]{2,1,0:T(8,128)(2,1)S(1)}, bf16[16,384,256]{2,1,0:T(8,128)(2,1)}, u32[]{:S(2)}) copy-start(bf16[16,384,256]{2,1,0:T(8,128)(2,1)} %site_ref.5) | copy-start | bytes 9437188
  2.7 0.7 copy-start.1
  10.4 1.8 %collective-permute-start = (bf16[2,384,256]{2,1,0:T(8,128)(2,1)S(1)}, bf16[2,384,256]{2,1,0:T(8,128)(2,1)S(1)}, u32[]{:S(2)}, u32[]{:S(2)}) collective-permute-start(bf16[2,384,256]{2,1,0:T(8,128)(2,1)S(1)} %get-tuple-element.16), channel_id=1, source_target_pairs={{0,16},{16,0},{32,48},{48,32},{64,80},{80,64},{96,112},{112,96},{1... | collective-permute-start | bytes 1179656 | tf_op jit(solution)/shard_map/ppermute | solution.py:245
  12.2 4.3 %collective-permute-start.1 = (bf16[4,384,256]{2,1,0:T(8,128)(2,1)S(1)}, bf16[4,384,256]{2,1,0:T(8,128)(2,1)S(1)}, u32[]{:S(2)}, u32[]{:S(2)}) collective-permute-start(bf16[4,384,256]{2,1,0:T(8,128)(2,1)S(1)} %get-tuple-element.17), channel_id=1, source_target_pairs={{0,16},{16,0},{32,48},{48,32},{64,80},{80,64},{96,112},{112,96},{1... | collective-permute-start | bytes 2359304 | tf_op jit(solution)/shard_map/ppermute | solution.py:247
  12.4 16.6 %collective-permute-start.3 = (bf16[2,384,256]{2,1,0:T(8,128)(2,1)S(1)}, bf16[2,384,256]{2,1,0:T(8,128)(2,1)S(1)}, u32[]{:S(2)}, u32[]{:S(2)}) collective-permute-start(bf16[2,384,256]{2,1,0:T(8,128)(2,1)S(1)} %add_convert_fusion), channel_id=1, source_target_pairs={{0,64},{16,80},{32,96},{48,112},{64,0},{80,16},{96,32},{112,48},{1... | collective-permute-start | bytes 1179656 | tf_op jit(solution)/shard_map/ppermute | solution.py:249
  22.3 12.4 %collective-permute-start.4 = (bf16[2,384,256]{2,1,0:T(8,128)(2,1)S(1)}, bf16[2,384,256]{2,1,0:T(8,128)(2,1)S(1)}, u32[]{:S(2)}, u32[]{:S(2)}) collective-permute-start(bf16[2,384,256]{2,1,0:T(8,128)(2,1)S(1)} %get-tuple-element.23), channel_id=1, source_target_pairs={{0,32},{16,48},{32,64},{48,80},{64,96},{80,112},{96,0},{112,16},{1... | collective-permute-start | bytes 1179656 | tf_op jit(solution)/shard_map/ppermute | solution.py:257
  23.4 11.3 %collective-permute-start.2 = (bf16[2,384,256]{2,1,0:T(8,128)(2,1)S(1)}, bf16[2,384,256]{2,1,0:T(8,128)(2,1)S(1)}, u32[]{:S(2)}, u32[]{:S(2)}) collective-permute-start(bf16[2,384,256]{2,1,0:T(8,128)(2,1)S(1)} %get-tuple-element.20), channel_id=1, source_target_pairs={{0,16},{16,0},{32,48},{48,32},{64,80},{80,64},{96,112},{112,96},{1... | collective-permute-start | bytes 1179656 | tf_op jit(solution)/shard_map/ppermute | solution.py:259
  23.4 35.4 %copy-start.2 = (s32[16]{0:T(128)S(1)}, s32[16]{0:T(128)}, u32[]{:S(2)}) copy-start(s32[16]{0:T(128)} %param.9) | copy-start | bytes 196
  23.4 11.9 %collective-permute-start.5 = (bf16[2,384,256]{2,1,0:T(8,128)(2,1)S(1)}, bf16[2,384,256]{2,1,0:T(8,128)(2,1)S(1)}, u32[]{:S(2)}, u32[]{:S(2)}) collective-permute-start(bf16[2,384,256]{2,1,0:T(8,128)(2,1)S(1)} %get-tuple-element.24), channel_id=1, source_target_pairs={{0,96},{16,112},{32,0},{48,16},{64,32},{80,48},{96,64},{112,80},{1... | collective-permute-start | bytes 1179656 | tf_op jit(solution)/shard_map/ppermute | solution.py:258
  51.8 16.7 %all-to-all-start.1 = ((bf16[16,48,256]{2,1,0:T(8,128)(2,1)}), bf16[16,48,256]{2,1,0:T(8,128)(2,1)S(1)}, u32[]{:S(2)}, u32[]{:S(2)}) async-start(bf16[16,48,256]{2,1,0:T(8,128)(2,1)} %bitcast.1), calls=%async_computation.1 | async-start | bytes 786432 | tf_op jit(solution)/shard_map/all_to_all | solution.py:264

commit v6 on v5

--- a/solution.py
+++ b/solution.py
@@ -262,6 +262,7 @@
     rows = lax.all_to_all(result, "mpo", split_axis=0, concat_axis=0, tiled=True)
     rows = rows.reshape(-1, rows.shape[2], columns)
     routed = lax.all_to_all(rows, "sec", split_axis=0, concat_axis=0, tiled=True)
+    routed, kept = lax.optimization_barrier((routed, kept))
     keep = jnp.arange(columns, dtype=jnp.int32)[None, None, :] < kept[:, None, None]
     return jnp.where(keep, routed, jnp.zeros((), BF16))
 

time: 69.6 us -> 69.3 us (level)
  blocking collectives: 13.2 us -> 29.6 us
  waiting for transfers between devices: 17.5 us -> 7.95 us
  starting transfers between devices: 14.6 us -> 7.58 us
    all_to_all x0 -> x1, blocking collectives: none -> 16.5 us  [shards(): lax.all_to_all(rows, 'sec', split_axis=0, concat_axis=0, tiled=True)]
    all_to_all x1 -> x0, waiting for transfers between devices: 9.54 us -> none  [shards(): lax.all_to_all(rows, 'sec', split_axis=0, concat_axis=0, tiled=True)]
    all_to_all x1 -> x0, starting transfers between devices: 7.03 us -> none  [shards(): lax.all_to_all(rows, 'sec', split_axis=0, concat_axis=0, tiled=True)]
  transfers between devices with their start and end apart: 7 -> 6, of which waited for: 4 -> 3; matrix products, arithmetic and copies ran while one was open for 0% -> 0% of each run, Pallas kernels for 13% -> 13%
where the time goes in v6:
time: 69.3 us; the launch traced here: 69 us
  blocking collectives  29.6 us (43%)
  Pallas kernels  19.5 us (28%)
  waiting for transfers between devices  7.95 us (11%)
  starting transfers between devices  7.58 us (11%)
  local copies, waits for them, and re-layouts  3.32 us (5%)
  other arithmetic  0.95 us (1%)
    all_to_all x1, blocking collectives, shards(): lax.all_to_all(rows, 'sec', split_axis=0, concat_axis=0, tiled=True)  16.5 us
    pallas_call x3, Pallas kernels, terms(): pl.pallas_call(functools.partial(term_kernel, groups=[(targets, dtype, ot...  16.2 us
    all_to_all x1, blocking collectives, shards(): lax.all_to_all(result, 'mpo', split_axis=0, concat_axis=0, tiled=True)  13.1 us
    ppermute x1, waiting for transfers between devices, shards(): up = lax.ppermute(up, 'mpo', shift(1))  5.65 us
    ppermute x1, starting transfers between devices, shards(): far = lax.ppermute(far, 'mpo', shift(2))  4.05 us
    pallas_call x1, Pallas kernels, expansions(): pl.pallas_call(root_kernel, out_shape=jax.ShapeDtypeStruct((parts, count,...  3.3 us
    unnamed x6, local copies, waits for them, and re-layouts  2.54 us
    ppermute x1, starting transfers between devices, shards(): down = lax.ppermute(down, 'mpo', shift(3))  2.22 us
  transfers between devices with their start and end apart: 6, of which 3 were waited for; matrix products, arithmetic and copies ran while one was open for 0% of the time, Pallas kernels for 13%

profile of v6, /device:TPU:0, one launch (start us, length us, event | category | flops | bytes accessed | tf_op | source)
XLA Modules:
  0.0 69.0 jit_solution(9660072753587526429)
XLA Ops:
  0.0 0.8 %reshape.37.mpo_ref = f32[64]{0:T(128)S(1)} reshape(bf16[4,4,4]{2,1,0:T(4,128)(2,1)} %param.7) | data formatting | bytes 384 | tf_op jit(solution)/shard_map/reshape | solution.py:233
  0.8 0.0 copy-start
  0.8 1.9 %copy-done = bf16[16,384,256]{2,1,0:T(8,128)(2,1)S(1)} copy-done((bf16[16,384,256]{2,1,0:T(8,128)(2,1)S(1)}, bf16[16,384,256]{2,1,0:T(8,128)(2,1)}, u32[]{:S(2)}) %copy-start) | copy-done | bytes 3145752
  2.7 0.0 copy-start.1
  2.7 0.7 copy-done.1
  3.3 7.0 %shard_map.55 = (bf16[2,384,256]{2,1,0:T(8,128)(2,1)S(1)}, bf16[4,384,256]{2,1,0:T(8,128)(2,1)S(1)}, f32[2,384,256]{2,1,0:T(8,128)S(1)}) custom-call(s32[1]{0:T(128)} %bitcast.me_ref, s32[16]{0:T(128)S(1)} %copy-done.1, f32[64]{0:T(128)S(1)} %reshape.37.mpo_ref, bf16[16,4,384,384]{3,2,1,0:T(8,128)(2,1)} %left_hbm.5, bf16[16,384,256]{2,1,0:T(8,128)(2,1)S(1)} %copy-done), custom_call_target="tpu_custom_call" | custom-call | flops 4026531840 | bytes 11010048 | tf_op jit(solution)/shard_map/pallas_call | solution.py:91
  10.4 0.1 collective-permute-start
  10.5 1.7 %collective-permute-done = bf16[2,384,256]{2,1,0:T(8,128)(2,1)S(1)} collective-permute-done((bf16[2,384,256]{2,1,0:T(8,128)(2,1)S(1)}, bf16[2,384,256]{2,1,0:T(8,128)(2,1)S(1)}, u32[]{:S(2)}, u32[]{:S(2)}) %collective-permute-start) | collective-permute-done | bytes 393248 | tf_op jit(solution)/shard_map/ppermute | solution.py:245
  12.2 0.1 collective-permute-start.1
  12.3 0.1 add_convert_fusion
  12.4 4.1 %collective-permute-start.3 = (bf16[2,384,256]{2,1,0:T(8,128)(2,1)S(1)}, bf16[2,384,256]{2,1,0:T(8,128)(2,1)S(1)}, u32[]{:S(2)}, u32[]{:S(2)}) collective-permute-start(bf16[2,384,256]{2,1,0:T(8,128)(2,1)S(1)} %add_convert_fusion), channel_id=1, source_target_pairs={{0,64},{16,80},{32,96},{48,112},{64,0},{80,16},{96,32},{112,48},{1... | collective-permute-start | bytes 1179656 | tf_op jit(solution)/shard_map/ppermute | solution.py:249
  16.5 0.0 collective-permute-done.1.rest_0_.rest_1_
  16.5 5.8 %shard_map.56 = (bf16[2,384,256]{2,1,0:T(8,128)(2,1)S(1)}, bf16[2,384,256]{2,1,0:T(8,128)(2,1)S(1)}, bf16[2,384,256]{2,1,0:T(8,128)(2,1)S(1)}) custom-call(s32[1]{0:T(128)} %bitcast.me_ref, s32[16]{0:T(128)S(1)} %copy-done.1, f32[64]{0:T(128)S(1)} %reshape.37.mpo_ref, bf16[16,4,384,384]{3,2,1,0:T(8,128)(2,1)} %left_hbm.5, bf16[16,384,256]{2,1,0:T(8,128)(2,1)S(1)} %copy-done, ...), custom_call_target="tpu_custom_call" | custom-call | flops 3019898880 | bytes 8257536 | tf_op jit(solution)/shard_map/pallas_call | solution.py:91
  22.3 1.1 %collective-permute-start.4 = (bf16[2,384,256]{2,1,0:T(8,128)(2,1)S(1)}, bf16[2,384,256]{2,1,0:T(8,128)(2,1)S(1)}, u32[]{:S(2)}, u32[]{:S(2)}) collective-permute-start(bf16[2,384,256]{2,1,0:T(8,128)(2,1)S(1)} %get-tuple-element.25), channel_id=1, source_target_pairs={{0,32},{16,48},{32,64},{48,80},{64,96},{80,112},{96,0},{112,16},{1... | collective-permute-start | bytes 1179656 | tf_op jit(solution)/shard_map/ppermute | solution.py:257
  23.4 0.0 collective-permute-start.2
  23.4 0.0 copy-start.2
  23.4 2.2 %collective-permute-start.5 = (bf16[2,384,256]{2,1,0:T(8,128)(2,1)S(1)}, bf16[2,384,256]{2,1,0:T(8,128)(2,1)S(1)}, u32[]{:S(2)}, u32[]{:S(2)}) collective-permute-start(bf16[2,384,256]{2,1,0:T(8,128)(2,1)S(1)} %get-tuple-element.26), channel_id=1, source_target_pairs={{0,96},{16,112},{32,0},{48,16},{64,32},{80,48},{96,64},{112,80},{1... | collective-permute-start | bytes 1179656 | tf_op jit(solution)/shard_map/ppermute | solution.py:258
  25.6 3.4 %shard_map.57.own_ref = f32[2,384,256]{2,1,0:T(8,128)S(1)} custom-call(s32[1]{0:T(128)} %bitcast.me_ref, s32[16]{0:T(128)S(1)} %copy-done.1, f32[64]{0:T(128)S(1)} %reshape.37.mpo_ref, bf16[16,4,384,384]{3,2,1,0:T(8,128)(2,1)} %left_hbm.5, bf16[16,384,256]{2,1,0:T(8,128)(2,1)S(1)} %copy-done), custom_call_target="tpu_custom_call" | custom-call | flops 1006632960 | bytes 2752512 | tf_op jit(solution)/shard_map/pallas_call | solution.py:91
  29.0 0.0 collective-permute-done.3.far_ref
  29.0 5.7 %collective-permute-done.4.up_ref = bf16[2,384,256]{2,1,0:T(8,128)(2,1)S(1)} collective-permute-done((bf16[2,384,256]{2,1,0:T(8,128)(2,1)S(1)}, bf16[2,384,256]{2,1,0:T(8,128)(2,1)S(1)}, u32[]{:S(2)}, u32[]{:S(2)}) %collective-permute-start.4) | collective-permute-done | bytes 393248 | tf_op jit(solution)/shard_map/ppermute | solution.py:257
  34.7 0.0 collective-permute-done.2.other_ref
  34.7 0.6 collective-permute-done.5.down_ref
  35.3 3.3 %shard_map.58 = bf16[8,2,48,256]{3,2,1,0:T(8,128)(2,1)S(1)} custom-call(f32[2,384,256]{2,1,0:T(8,128)S(1)} %shard_map.57.own_ref, bf16[2,384,256]{2,1,0:T(8,128)(2,1)S(1)} %collective-permute-done.2.other_ref, bf16[2,384,256]{2,1,0:T(8,128)(2,1)S(1)} %collective-permute-done.3.far_ref, bf16[2,384,256]{2,1,0:T(8,128)(2,1)S(1)} %collective-permute-done.4.up_ref, ...), custom_call_target="tpu_custom_call" | custom-call | flops 3623878656 | bytes 2359296 | tf_op jit(solution)/shard_map/pallas_call | solution.py:210
  38.6 13.1 %all_to_all.10 = bf16[8,2,48,256]{3,2,1,0:T(8,128)(2,1)S(1)} all-to-all(bf16[8,2,48,256]{3,2,1,0:T(8,128)(2,1)S(1)} %shard_map.58), channel_id=1, replica_groups=mesh['mpo'=8,'sec'=16] {'mpo'}, dimensions={0} | all-to-all | bytes 786432 | tf_op jit(solution)/shard_map/all_to_all | solution.py:262
  51.7 16.5 %all_to_all.11 = bf16[16,48,256]{2,1,0:T(8,128)(2,1)S(1)} all-to-all(bf16[16,48,256]{2,1,0:T(8,128)(2,1)S(1)} %bitcast.2), channel_id=1, replica_groups=mesh['mpo'=8,'sec'=16] {'sec'}, dimensions={0} | all-to-all | bytes 786432 | tf_op jit(solution)/shard_map/all_to_all | solution.py:264
  68.1 0.0 copy-done.2
  68.1 0.1 iota_compare_fusion
  68.2 0.8 %broadcast_select_fusion = bf16[16,48,256]{2,1,0:T(8,128)(2,1)} fusion(bf16[16,48,256]{2,1,0:T(8,128)(2,1)S(1)} %all_to_all.11, pred[16,256]{1,0:T(8,128)(4,1)S(1)} %iota_compare_fusion), kind=kLoop, calls=%fused_computation.1 | loop fusion | flops 196608 | bytes 790528 | tf_op jit(solution)/shard_map/jit(_where)/select_n | solution.py:267
Async XLA Ops:
  0.8 1.9 %copy-start = (bf16[16,384,256]{2,1,0:T(8,128)(2,1)S(1)}, bf16[16,384,256]{2,1,0:T(8,128)(2,1)}, u32[]{:S(2)}) copy-start(bf16[16,384,256]{2,1,0:T(8,128)(2,1)} %site_ref.5) | copy-start | bytes 9437188
  2.7 0.7 copy-start.1
  10.4 1.8 %collective-permute-start = (bf16[2,384,256]{2,1,0:T(8,128)(2,1)S(1)}, bf16[2,384,256]{2,1,0:T(8,128)(2,1)S(1)}, u32[]{:S(2)}, u32[]{:S(2)}) collective-permute-start(bf16[2,384,256]{2,1,0:T(8,128)(2,1)S(1)} %get-tuple-element.18), channel_id=1, source_target_pairs={{0,16},{16,0},{32,48},{48,32},{64,80},{80,64},{96,112},{112,96},{1... | collective-permute-start | bytes 1179656 | tf_op jit(solution)/shard_map/ppermute | solution.py:245
  12.2 4.3 %collective-permute-start.1 = (bf16[4,384,256]{2,1,0:T(8,128)(2,1)S(1)}, bf16[4,384,256]{2,1,0:T(8,128)(2,1)S(1)}, u32[]{:S(2)}, u32[]{:S(2)}) collective-permute-start(bf16[4,384,256]{2,1,0:T(8,128)(2,1)S(1)} %get-tuple-element.19), channel_id=1, source_target_pairs={{0,16},{16,0},{32,48},{48,32},{64,80},{80,64},{96,112},{112,96},{1... | collective-permute-start | bytes 2359304 | tf_op jit(solution)/shard_map/ppermute | solution.py:247
  12.4 16.6 %collective-permute-start.3 = (bf16[2,384,256]{2,1,0:T(8,128)(2,1)S(1)}, bf16[2,384,256]{2,1,0:T(8,128)(2,1)S(1)}, u32[]{:S(2)}, u32[]{:S(2)}) collective-permute-start(bf16[2,384,256]{2,1,0:T(8,128)(2,1)S(1)} %add_convert_fusion), channel_id=1, source_target_pairs={{0,64},{16,80},{32,96},{48,112},{64,0},{80,16},{96,32},{112,48},{1... | collective-permute-start | bytes 1179656 | tf_op jit(solution)/shard_map/ppermute | solution.py:249
  22.3 12.4 %collective-permute-start.4 = (bf16[2,384,256]{2,1,0:T(8,128)(2,1)S(1)}, bf16[2,384,256]{2,1,0:T(8,128)(2,1)S(1)}, u32[]{:S(2)}, u32[]{:S(2)}) collective-permute-start(bf16[2,384,256]{2,1,0:T(8,128)(2,1)S(1)} %get-tuple-element.25), channel_id=1, source_target_pairs={{0,32},{16,48},{32,64},{48,80},{64,96},{80,112},{96,0},{112,16},{1... | collective-permute-start | bytes 1179656 | tf_op jit(solution)/shard_map/ppermute | solution.py:257
  23.4 11.3 %collective-permute-start.2 = (bf16[2,384,256]{2,1,0:T(8,128)(2,1)S(1)}, bf16[2,384,256]{2,1,0:T(8,128)(2,1)S(1)}, u32[]{:S(2)}, u32[]{:S(2)}) collective-permute-start(bf16[2,384,256]{2,1,0:T(8,128)(2,1)S(1)} %get-tuple-element.22), channel_id=1, source_target_pairs={{0,16},{16,0},{32,48},{48,32},{64,80},{80,64},{96,112},{112,96},{1... | collective-permute-start | bytes 1179656 | tf_op jit(solution)/shard_map/ppermute | solution.py:259
  23.4 44.7 %copy-start.2 = (s32[16]{0:T(128)S(1)}, s32[16]{0:T(128)}, u32[]{:S(2)}) copy-start(s32[16]{0:T(128)} %param.9) | copy-start | bytes 196
  23.4 11.9 %collective-permute-start.5 = (bf16[2,384,256]{2,1,0:T(8,128)(2,1)S(1)}, bf16[2,384,256]{2,1,0:T(8,128)(2,1)S(1)}, u32[]{:S(2)}, u32[]{:S(2)}) collective-permute-start(bf16[2,384,256]{2,1,0:T(8,128)(2,1)S(1)} %get-tuple-element.26), channel_id=1, source_target_pairs={{0,96},{16,112},{32,0},{48,16},{64,32},{80,48},{96,64},{112,80},{1... | collective-permute-start | bytes 1179656 | tf_op jit(solution)/shard_map/ppermute | solution.py:258
